TPU v7x, 128 devices: a whole 4x4x4 slice. The times are simulated.
128 devices in a mesh: batch: 16 (over y, x), seq: 8 (over z, core).
Axes of the slice: x: 4, y: 4, z: 4, core: 2. Of those that a mesh axis runs over, the one named last changes fastest.
Arguments:
- block_input: bfloat16 [64, 1024, 768], P('batch', 'seq'), may hold values from -6 to 6
- token_ids: int32 [64, 1024], P('batch', 'seq'), may hold values from 0 to 8007, as said below
- hash_table: int32 [8008], replicated, may hold values from 0 to 15
- doc_lengths: int32 [64, 8], P('batch'), may hold values from 1 to 256, 1024 in all within a row
- turn_mask: int32 [64, 1024], P('batch', 'seq'), may hold values 0 or 1
- attn_norm_gain: float32 [768], replicated, may hold values from 0.5 to 1.5
- attn_norm_bias: float32 [768], replicated, may hold values from -3 to 3
- qkv_weight: bfloat16 [768, 2304], replicated, may hold values from -0.21875 to 0.21875
- proj_weight: bfloat16 [768, 768], replicated, may hold values from -1.75 to 1.75
- ffn_norm_gain: float32 [768], replicated, may hold values from 0.5 to 1.5
- ffn_norm_bias: float32 [768], replicated, may hold values from -3 to 3
- expert_up: bfloat16 [16, 768, 3072], P('batch'), may hold values from -0.21875 to 0.21875
- expert_down: bfloat16 [16, 3072, 768], P('batch'), may hold values from -0.109375 to 0.109375
- out_grad: bfloat16 [64, 1024, 768], P('batch', 'seq'), may hold values from -6 to 6
Outputs:
- block_output: bfloat16 [64, 1024, 768], P('batch', 'seq')
- input_grad: float32 [64, 1024, 768], P('batch', 'seq')
- attn_gain_grad: float32 [768], replicated
- attn_bias_grad: float32 [768], replicated
- qkv_grad: float32 [768, 2304], replicated
- proj_grad: float32 [768, 768], replicated
- ffn_gain_grad: float32 [768], replicated
- ffn_bias_grad: float32 [768], replicated
- up_grad: float32 [16, 768, 3072], P('batch', None, 'seq')
- down_grad: float32 [16, 3072, 768], P('batch', 'seq')
- expert_counts: int32 [16], replicated
- received_counts: int32 [16, 8, 16], P('batch', 'seq')
Inputs may be any that keep to these rules, and one draw needn't show every extreme that they name: `token_ids`: among the 512 tokens of one device (4 rows by 128 positions), at most 64 have an expert (by hash_table) equal to any one expert; in every draw one expert gets exactly 64 from every device. `doc_lengths`: the 8 lengths of a row sum to 1024; the longest of each row is exactly 256.
All inputs are finite; a program needn't handle non-finite values. No bound on the sum of `turn_mask` on one device may be relied on, other than what follows from the above.
Results may differ from a plain program's by a relative error of at most 0.0098.
Values may be sent and summed in bfloat16 or wider, within the bound.
No kernel may reach another device: no remote copies, remote signals or barrier semaphores. Data moves between devices by JAX's collectives and lax.ppermute only.
A program may use at most 192 MiB of HBM per device.

v0:
```python
import jax
import jax.numpy as jnp
from jax import lax
from jax.sharding import PartitionSpec as P

HEADS = 12
MAXLEN = 256


EPS = 1e-05
MASKED = -1e30


def from_behind(block, axis, distance):
    devices = range(lax.axis_size(axis))
    route = [(i - distance, i) for i in devices if i - distance in devices]
    return lax.ppermute(block, axis, route)


def layer_norm(values, gain_vec, bias_vec):
    row_mean = jnp.mean(values, axis=-1, keepdims=True)
    centred = values - row_mean
    spread = jnp.mean(centred * centred, axis=-1, keepdims=True)
    return centred * lax.rsqrt(spread + EPS) * gain_vec + bias_vec


def gelu_curve(values):
    return jax.nn.gelu(values, approximate=True)


def inner_rows(left_side, right_side):
    return lax.dot_general(
        left_side, right_side, (((0,), (0,)), ((), ())), preferred_element_type=jnp.float32
    )


def times_transposed(left_side, right_side):
    return lax.dot_general(
        left_side, right_side, (((1,), (1,)), ((), ())), preferred_element_type=jnp.float32
    )


def segment_of(positions, doc_lengths):
    doc_ends = jnp.cumsum(doc_lengths, axis=-1)
    return jnp.sum((positions[None, :, None] >= doc_ends[:, None, :]).astype(jnp.int32), axis=-1)


def local(
    block_input,
    token_ids,
    hash_table,
    doc_lengths,
    turn_mask,
    attn_norm_gain,
    attn_norm_bias,
    qkv_weight,
    proj_weight,
    ffn_norm_gain,
    ffn_norm_bias,
    expert_up,
    expert_down,
    out_grad,
):
    row_count, shard_len, model_width = block_input.shape
    tokens_here = row_count * shard_len
    owners = lax.axis_size("batch")
    seq_count = lax.axis_size("seq")
    seq_place = lax.axis_index("seq")
    owner_place = lax.axis_index("batch")
    capacity = 2 * tokens_here // owners
    head_count = HEADS
    head_size = model_width // head_count
    score_scale = head_size ** (-0.5)
    hop_count = min(-(-(MAXLEN - 1) // shard_len), seq_count - 1)
    key_span = (hop_count + 1) * shard_len
    up_matrix = expert_up[0]
    down_matrix = expert_down[0]
    inputs = block_input.astype(jnp.float32)
    normed_one = (
        layer_norm(inputs, attn_norm_gain, attn_norm_bias)
        .astype(jnp.bfloat16)
        .reshape(tokens_here, model_width)
    )
    projected = jnp.dot(normed_one, qkv_weight, preferred_element_type=jnp.float32).astype(
        jnp.bfloat16
    )
    projected = projected.reshape(row_count, shard_len, 3 * model_width)
    keyvals = projected[..., model_width:]
    earlier = []
    for distance in range(hop_count, 0, -1):
        earlier.append(from_behind(keyvals, "seq", distance))
    context = jnp.concatenate(earlier + [keyvals], axis=1)
    query_pos = seq_place * shard_len + jnp.arange(shard_len, dtype=jnp.int32)
    key_pos = (seq_place - hop_count) * shard_len + jnp.arange(key_span, dtype=jnp.int32)
    query_seg = segment_of(query_pos, doc_lengths)
    key_seg = segment_of(key_pos, doc_lengths)
    allowed = (
        (query_seg[:, :, None] == key_seg[:, None, :])
        & (key_pos[None, None, :] <= query_pos[None, :, None])
        & (key_pos >= 0)[None, None, :]
    )
    query_heads = projected[..., :model_width].reshape(row_count, shard_len, head_count, head_size)
    key_heads = context[..., :model_width].reshape(row_count, key_span, head_count, head_size)
    value_heads = context[..., model_width:].reshape(row_count, key_span, head_count, head_size)

    def scores_of():
        scores = (
            jnp.einsum(
                "rqhd,rkhd->rhqk", query_heads, key_heads, preferred_element_type=jnp.float32
            )
            * score_scale
        )
        return jnp.where(allowed[:, None], scores, MASKED)

    scores = scores_of()
    row_top = jnp.max(scores, axis=-1, keepdims=True)
    weights = jnp.exp(scores - row_top)
    row_total = jnp.sum(weights, axis=-1, keepdims=True)
    attention = weights / row_total
    log_total = row_top + jnp.log(row_total)
    attended = jnp.einsum(
        "rhqk,rkhd->rqhd",
        attention.astype(jnp.bfloat16),
        value_heads,
        preferred_element_type=jnp.float32,
    )
    attended = attended.astype(jnp.bfloat16).reshape(tokens_here, model_width)
    mixed_out = jnp.dot(attended, proj_weight, preferred_element_type=jnp.float32).reshape(
        row_count, shard_len, model_width
    )
    after_attn = inputs + mixed_out
    normed_two = (
        layer_norm(after_attn, ffn_norm_gain, ffn_norm_bias)
        .astype(jnp.bfloat16)
        .reshape(tokens_here, model_width)
    )
    chosen = hash_table[token_ids.reshape(-1)]
    member = (chosen[:, None] == jnp.arange(owners, dtype=jnp.int32)[None, :]).astype(jnp.int32)
    before = jnp.cumsum(member, axis=0) - member
    slot_index = jnp.sum(before * member, axis=1)
    target = chosen * capacity + slot_index
    placing = (jnp.arange(owners * capacity, dtype=jnp.int32)[:, None] == target[None, :]).astype(
        jnp.bfloat16
    )
    send_counts = jnp.sum(member, axis=0).reshape(owners, 1)
    got_counts = lax.all_to_all(send_counts, "batch", split_axis=0, concat_axis=0, tiled=True)
    outgoing = jnp.dot(placing, normed_two, preferred_element_type=jnp.float32).astype(jnp.bfloat16)
    outgoing = outgoing.reshape(owners, capacity, model_width)
    arrived = lax.all_to_all(outgoing, "batch", split_axis=0, concat_axis=0, tiled=True)
    item_count = arrived.shape[1]
    flat_rows = arrived.reshape(owners * item_count, model_width)
    hidden = jnp.dot(flat_rows, up_matrix, preferred_element_type=jnp.float32)
    active = gelu_curve(hidden).astype(jnp.bfloat16)
    result = jnp.dot(active, down_matrix, preferred_element_type=jnp.float32).astype(jnp.bfloat16)
    returned = lax.all_to_all(
        result.reshape(owners, item_count, model_width),
        "batch",
        split_axis=0,
        concat_axis=0,
        tiled=True,
    )
    outcome = (returned, arrived, hidden.reshape(owners, item_count, hidden.shape[1]))
    returned = outcome[0]
    arrived_flat = outcome[1].reshape(owners * capacity, model_width)
    expert_out = inner_rows(placing, returned.reshape(owners * capacity, model_width))
    block_output = (after_attn + expert_out.reshape(row_count, shard_len, model_width)).astype(
        jnp.bfloat16
    )
    upstream = out_grad.astype(jnp.float32) * turn_mask.astype(jnp.float32)[..., None]
    upstream_low = upstream.astype(jnp.bfloat16).reshape(tokens_here, model_width)
    grad_out = jnp.dot(placing, upstream_low, preferred_element_type=jnp.float32).astype(
        jnp.bfloat16
    )
    grad_arrived = lax.all_to_all(
        grad_out.reshape(owners, capacity, model_width),
        "batch",
        split_axis=0,
        concat_axis=0,
        tiled=True,
    )
    grad_arrived = grad_arrived.reshape(owners * capacity, model_width)
    hidden = outcome[2].reshape(owners * capacity, up_matrix.shape[1])
    active, gelu_pull = jax.vjp(gelu_curve, hidden)
    down_local = inner_rows(active.astype(jnp.bfloat16), grad_arrived)
    active_grad = times_transposed(grad_arrived, down_matrix)
    hidden_grad = gelu_pull(active_grad)[0].astype(jnp.bfloat16)
    up_local = inner_rows(arrived_flat, hidden_grad)
    sent_grad = times_transposed(hidden_grad, up_matrix).astype(jnp.bfloat16)
    back_grad = lax.all_to_all(
        sent_grad.reshape(owners, capacity, model_width),
        "batch",
        split_axis=0,
        concat_axis=0,
        tiled=True,
    )
    normed_two_grad = inner_rows(placing, back_grad.reshape(owners * capacity, model_width))
    normed_two_grad = normed_two_grad.reshape(row_count, shard_len, model_width)
    norm_two_out, norm_two_pull = jax.vjp(layer_norm, after_attn, ffn_norm_gain, ffn_norm_bias)
    residual_two, gain_two_grad, bias_two_grad = norm_two_pull(normed_two_grad)
    after_grad = upstream + residual_two
    mixed_grad = after_grad.astype(jnp.bfloat16).reshape(tokens_here, model_width)
    proj_local = inner_rows(attended, mixed_grad)
    attended_grad = times_transposed(mixed_grad, proj_weight).astype(jnp.bfloat16)
    attended_grad = attended_grad.reshape(row_count, shard_len, head_count, head_size)
    attention = jnp.exp(scores_of() - log_total)
    prob_grad = jnp.einsum(
        "rqhd,rkhd->rhqk", attended_grad, value_heads, preferred_element_type=jnp.float32
    )
    score_grad = attention * (prob_grad - jnp.sum(attention * prob_grad, axis=-1, keepdims=True))
    score_grad = score_grad.astype(jnp.bfloat16)
    query_grad = (
        jnp.einsum("rhqk,rkhd->rqhd", score_grad, key_heads, preferred_element_type=jnp.float32)
        * score_scale
    )
    key_grad = (
        jnp.einsum("rhqk,rqhd->rkhd", score_grad, query_heads, preferred_element_type=jnp.float32)
        * score_scale
    )
    value_grad = jnp.einsum(
        "rhqk,rqhd->rkhd",
        attention.astype(jnp.bfloat16),
        attended_grad,
        preferred_element_type=jnp.float32,
    )
    context_grad = jnp.concatenate(
        [
            key_grad.reshape(row_count, key_span, model_width),
            value_grad.reshape(row_count, key_span, model_width),
        ],
        axis=-1,
    )
    own_grad = context_grad[:, hop_count * shard_len :]
    for distance in range(hop_count, 0, -1):
        offset_rows = (hop_count - distance) * shard_len
        own_grad = own_grad + from_behind(
            context_grad[:, offset_rows : offset_rows + shard_len], "seq", -distance
        )
    projected_grad = jnp.concatenate(
        [query_grad.reshape(row_count, shard_len, model_width), own_grad], axis=-1
    )
    projected_grad = projected_grad.astype(jnp.bfloat16).reshape(tokens_here, 3 * model_width)
    qkv_local = inner_rows(normed_one, projected_grad)
    normed_one_grad = times_transposed(projected_grad, qkv_weight).reshape(
        row_count, shard_len, model_width
    )
    norm_one_out, norm_one_pull = jax.vjp(layer_norm, inputs, attn_norm_gain, attn_norm_bias)
    residual_one, gain_one_grad, bias_one_grad = norm_one_pull(normed_one_grad)
    input_grad = after_grad + residual_one
    norm_terms = jnp.stack([gain_one_grad, bias_one_grad, gain_two_grad, bias_two_grad])
    arrived_total = jnp.sum(got_counts).astype(jnp.float32)
    count_terms = jnp.where(jnp.arange(owners, dtype=jnp.int32) == owner_place, arrived_total, 0.0)
    received_block = got_counts.reshape(1, 1, owners)
    up_term = up_local[None]
    down_term = down_local[None]
    up_sum, down_sum = (
        lax.psum_scatter(up_term, "seq", scatter_dimension=2, tiled=True),
        lax.psum_scatter(down_term, "seq", scatter_dimension=1, tiled=True),
    )
    qkv_sum, proj_sum, norm_sum, count_sum = lax.psum(
        (qkv_local, proj_local, norm_terms, count_terms), ("batch", "seq")
    )
    return (
        block_output,
        input_grad,
        norm_sum[0],
        norm_sum[1],
        qkv_sum,
        proj_sum,
        norm_sum[2],
        norm_sum[3],
        up_sum,
        down_sum,
        count_sum.astype(jnp.int32),
        received_block,
    )


def solution(mesh):
    placed = (
        P("batch", "seq", None),
        P("batch", "seq"),
        P(),
        P("batch", None),
        P("batch", "seq"),
        P(),
        P(),
        P(),
        P(),
        P(),
        P(),
        P("batch", None, None),
        P("batch", None, None),
        P("batch", "seq", None),
    )
    return jax.shard_map(
        local,
        mesh=mesh,
        in_specs=placed,
        out_specs=(
            P("batch", "seq", None),
            P("batch", "seq", None),
            P(),
            P(),
            P(),
            P(),
            P(),
            P(),
            P("batch", None, "seq"),
            P("batch", "seq", None),
            P(),
            P("batch", "seq", None),
        ),
        check_vma=False,
    )
```

profile of v0, /device:TPU:1, one launch (start us, length us, event | category | flops | bytes accessed | tf_op | source)
XLA Modules:
  0.0 588.4 jit_solution(8683451306485596627)
XLA Ops:
  9.5 1.5 fusion.49
  11.6 1.5 fusion.47
  13.1 2.0 convolution_convert_fusion
  17.8 5.1 collective-permute-start.1
  22.9 4.7 collective-permute-start
  27.6 3.4 gather_fusion
  31.7 2.1 slice.56
  33.9 3.1 reduce-window.6
  38.1 2.3 copy.78
  43.6 11.2 %collective-permute-done.1 = bf16[4,128,1536]{2,1,0:T(8,128)(2,1)} collective-permute-done((bf16[4,128,1536]{2,1,0:T(8,128)(2,1)}, bf16[4,128,1536]{2,1,0:T(8,128)(2,1)}, u32[]{:S(2)}, u32[]{:S(2)}) %collective-permute-start.1) | collective-permute-done | bytes 1572896 | tf_op jit(solution)/shard_map/ppermute | solution.py:17
  54.8 19.4 %collective-permute-done = bf16[4,128,1536]{2,1,0:T(8,128)(2,1)} collective-permute-done((bf16[4,128,1536]{2,1,0:T(8,128)(2,1)}, bf16[4,128,1536]{2,1,0:T(8,128)(2,1)}, u32[]{:S(2)}, u32[]{:S(2)}) %collective-permute-start) | collective-permute-done | bytes 1572896 | tf_op jit(solution)/shard_map/ppermute | solution.py:17
  74.2 2.5 pad_maximum_fusion
  76.7 2.5 fusion.73
  79.2 4.3 copy.79
  83.5 4.3 copy.77
  87.8 3.8 fusion.74
  91.7 2.4 fusion.7
  94.1 1.5 copy-done.1
  95.7 3.5 fusion.52
  100.8 2.2 fusion.38
  103.0 7.3 %all-to-all-start = ((bf16[16,64,768]{2,1,0:T(8,128)(2,1)}), bf16[16,64,768]{2,1,0:T(8,128)(2,1)}, u32[]{:S(2)}, u32[]{:S(2)}) async-start(bf16[16,64,768]{2,1,0:T(8,128)(2,1)} %bitcast.137), calls=%async_computation | async-start | bytes 3145728 | tf_op jit(solution)/shard_map/all_to_all | solution.py:149
  112.3 2.9 fusion.39
  115.2 13.5 %all-to-all-done = bf16[16,64,768]{2,1,0:T(8,128)(2,1)} async-done(((bf16[16,64,768]{2,1,0:T(8,128)(2,1)}), bf16[16,64,768]{2,1,0:T(8,128)(2,1)}, u32[]{:S(2)}, u32[]{:S(2)}) %all-to-all-start) | async-done | bytes 1572896 | tf_op jit(solution)/shard_map/all_to_all | solution.py:149
  128.7 4.4 all-to-all-start.2
  133.1 10.0 %fusion.17 = f32[1024,3072]{1,0:T(8,128)} fusion(bf16[1024,768]{1,0:T(8,128)(2,1)} %bitcast.15, bf16[1,768,3072]{2,1,0:T(8,128)(2,1)} %param.25), kind=kOutput, calls=%fused_computation.34 | convolution fusion | flops 4831838208 | bytes 18874368 | tf_op jit(solution)/shard_map/dot_general | solution.py:152
  143.1 6.2 %all-to-all-done.2 = bf16[16,64,768]{2,1,0:T(8,128)(2,1)} async-done(((bf16[16,64,768]{2,1,0:T(8,128)(2,1)}), bf16[16,64,768]{2,1,0:T(8,128)(2,1)}, u32[]{:S(2)}, u32[]{:S(2)}) %all-to-all-start.2) | async-done | bytes 1572896 | tf_op jit(solution)/shard_map/all_to_all | solution.py:174
  149.3 15.3 %fusion.6 = bf16[1024,3072]{1,0:T(8,128)(2,1)S(1)} fusion(f32[1024,3072]{1,0:T(8,128)} %fusion.17, bf16[1024,768]{1,0:T(8,128)(2,1)} %bitcast.23, bf16[1,3072,768]{2,1,0:T(8,128)(2,1)} %param.26), kind=kOutput, calls=%fused_computation.9 | convolution fusion | flops 4894752768 | bytes 25165824 | tf_op jit(solution)/shard_map/dot_general | solution.py:38
  164.7 10.8 %fusion.40 = bf16[1024,768]{1,0:T(8,128)(2,1)} fusion(bf16[1024,3072]{1,0:T(8,128)(2,1)S(1)} %fusion.6, bf16[1,768,3072]{2,1,0:T(8,128)(2,1)} %param.25), kind=kOutput, calls=%fused_computation.66 | convolution fusion | flops 4832624640 | bytes 12582912 | tf_op jit(solution)/shard_map/dot_general | solution.py:38
  175.5 4.4 all-to-all-start.3
  180.1 1.8 iota_compare_fusion.3
  183.3 12.7 %all-to-all-done.3 = bf16[16,64,768]{2,1,0:T(8,128)(2,1)} async-done(((bf16[16,64,768]{2,1,0:T(8,128)(2,1)}), bf16[16,64,768]{2,1,0:T(8,128)(2,1)}, u32[]{:S(2)}, u32[]{:S(2)}) %all-to-all-start.3) | async-done | bytes 1572896 | tf_op jit(solution)/shard_map/all_to_all | solution.py:189
  196.1 4.0 multiply_reduce_fusion.1
  203.1 1.7 convolution_convert_fusion.1
  204.8 2.3 copy.82
  207.1 2.4 reshape.347
  209.5 8.0 %fusion.9 = f32[4,12,64,384]{3,2,1,0:T(8,128)} fusion(f32[4,12,128,384]{3,2,1,0:T(8,128)} %copy-done.1, f32[4,12,128]{2,1,0:T(8,128)} %log_add_fusion, bf16[4,128,12,64]{1,0,3,2:T(4,128)(2,1)} %reshape.347), kind=kOutput, calls=%fused_computation.26 | convolution fusion | flops 306708480 | bytes 14966784 | tf_op jit(solution)/shard_map/rhqk,rqhd->rkhd/dot_general | solution.py:219
  217.5 8.4 %multiply_reduce_fusion = (f32[4,12,128]{2,1,0:T(8,128)}, f32[4,12,128,384]{3,2,1,0:T(8,128)}) fusion(f32[4,12,128,384]{3,2,1,0:T(8,128)} %copy-done.1, f32[4,12,128]{2,1,0:T(8,128)S(1)} %copy-done.29, bf16[4,384,12,64]{1,3,2,0:T(8,128)(2,1)S(1)} %bitcast.124, bf16[4,128,12,64]{1,0,3,2:T(4,128)(2,1)S(1)} %copy-done.13), kind=kOutput, calls=%fused_computation.16 | convolution fusion | flops 309061632 | bytes 22069248 | tf_op jit(solution)/shard_map/rqhd,rkhd->rhqk/dot_general | solution.py:206
  225.9 6.1 %copy.86 = f32[4,384,768]{2,1,0:T(8,128)} copy(f32[4,384,768]{1,2,0:T(8,128)} %bitcast.119) | data formatting | bytes 9437184 | tf_op jit(solution)/shard_map/reshape | solution.py:228
  232.0 7.5 %multiply_convert_fusion.1 = bf16[4,12,128,384]{3,2,1,0:T(8,128)(2,1)S(1)} fusion(f32[4,12,128,384]{3,2,1,0:T(8,128)} %get-tuple-element.42, f32[4,12,128,384]{3,2,1,0:T(8,128)} %copy-done.1, f32[4,12,128]{2,1,0:T(8,128)} %get-tuple-element.41, f32[4,12,128]{2,1,0:T(8,128)} %log_add_fusion), kind=kLoop, calls=%fused_computation.15 | loop fusion | flops 9437184 | bytes 23642112 | tf_op jit(solution)/shard_map/convert_element_type | solution.py:210
  239.5 3.6 broadcast_multiply_fusion
  243.0 6.1 %copy.85 = f32[4,384,768]{2,1,0:T(8,128)} copy(f32[4,384,768]{1,2,0:T(8,128)} %bitcast.120) | data formatting | bytes 9437184 | tf_op jit(solution)/shard_map/reshape | solution.py:227
  249.1 6.5 %fusion.25 = (f32[4,128,1536]{2,1,0:T(8,128)}, f32[4,128,1536]{2,1,0:T(8,128)}) fusion(f32[4,384,768]{2,1,0:T(8,128)} %copy.85, f32[4,384,768]{2,1,0:T(8,128)} %copy.86), kind=kLoop, calls=%fused_computation.41 | loop fusion | flops 1572864 | bytes 15728640 | tf_op jit(solution)/shard_map/concatenate | solution.py:225
  256.9 2.1 collective-permute-start.3
  259.0 1.5 copy.89
  260.5 3.1 multiply_convert_fusion.2
  263.6 2.3 copy.87
  265.9 3.6 fusion.57
  269.5 58.2 %collective-permute-done.2 = f32[4,128,1536]{2,1,0:T(8,128)} collective-permute-done((f32[4,128,1536]{2,1,0:T(8,128)}, f32[4,128,1536]{2,1,0:T(8,128)}, u32[]{:S(2)}, u32[]{:S(2)}) %collective-permute-start.2) | collective-permute-done | bytes 3145760 | tf_op jit(solution)/shard_map/ppermute | solution.py:17
  327.7 23.1 %collective-permute-done.3 = f32[4,128,1536]{2,1,0:T(8,128)} collective-permute-done((f32[4,128,1536]{2,1,0:T(8,128)}, f32[4,128,1536]{2,1,0:T(8,128)}, u32[]{:S(2)}, u32[]{:S(2)}) %collective-permute-start.3) | collective-permute-done | bytes 3145760 | tf_op jit(solution)/shard_map/ppermute | solution.py:17
  350.8 4.4 fusion.29
  356.4 5.0 convolution_bitcast_fusion
  361.5 12.8 %convolution_bitcast_fusion.1 = f32[1,3072,768]{2,1,0:T(8,128)} fusion(bf16[1024,768]{1,0:T(8,128)(2,1)} %bitcast.23, f32[1024,3072]{1,0:T(8,128)} %fusion.17), kind=kOutput, calls=%fused_computation.24 | convolution fusion | flops 4860149760 | bytes 23592960 | tf_op jit(solution)/shard_map/dot_general | solution.py:32
  374.4 10.1 %convolution_bitcast_fusion.2 = f32[1,768,3072]{2,1,0:T(8,128)} fusion(bf16[1024,768]{1,0:T(8,128)(2,1)} %bitcast.15, bf16[1024,3072]{1,0:T(8,128)(2,1)} %copy-done.53), kind=kOutput, calls=%fused_computation.25 | convolution fusion | flops 4831838208 | bytes 17301504 | tf_op jit(solution)/shard_map/dot_general | solution.py:32
  385.8 3.7 all-to-all-start.4
  389.5 12.9 %fusion.43 = bf16[1024,768]{1,0:T(8,128)(2,1)} fusion(bf16[1,3072,768]{2,1,0:T(8,128)(2,1)} %param.26, f32[1024,3072]{1,0:T(8,128)} %fusion.17), kind=kOutput, calls=%fused_computation.67 | convolution fusion | flops 4860936192 | bytes 18874368 | tf_op jit(solution)/shard_map/dot_general | solution.py:154
  402.4 6.9 %all-to-all-start.1 = ((bf16[16,64,768]{2,1,0:T(8,128)(2,1)}), bf16[16,64,768]{2,1,0:T(8,128)(2,1)}, u32[]{:S(2)}, u32[]{:S(2)}) async-start(bf16[16,64,768]{2,1,0:T(8,128)(2,1)} %bitcast.134), calls=%async_computation.1 | async-start | bytes 3145728 | tf_op jit(solution)/shard_map/all_to_all | solution.py:155
  412.6 13.7 %all-to-all-done.1 = bf16[16,64,768]{2,1,0:T(8,128)(2,1)} async-done(((bf16[16,64,768]{2,1,0:T(8,128)(2,1)}), bf16[16,64,768]{2,1,0:T(8,128)(2,1)}, u32[]{:S(2)}, u32[]{:S(2)}) %all-to-all-start.1) | async-done | bytes 1572896 | tf_op jit(solution)/shard_map/all_to_all | solution.py:155
  426.3 4.1 add_convert_fusion
  430.4 2.1 fusion.50
  434.1 76.4 %all-reduce = (f32[4,768]{1,0:T(4,128)}, f32[16]{0:T(128)}) all-reduce(f32[4,768]{1,0:T(4,128)S(1)} %pad_maximum_fusion.5, f32[16]{0:T(128)} %compare_select_fusion.1), channel_id=1, replica_groups=mesh['batch'=16,'seq'=8] {'batch','seq'}, use_global_device_ids=true, to_apply=%region_21.22 | all-reduce | flops 3088 | bytes 24704 | tf_op jit(solution)/shard_map/psum | solution.py:259
  511.7 1.5 slice_reduce_fusion.1
  513.9 3.7 add_add_fusion.2
  517.6 55.0 %all-reduce.4.cloned.1.call-done = (f32[768,2304]{1,0:T(8,128)}, f32[768,768]{1,0:T(8,128)}) async-done(((f32[768,2304]{1,0:T(8,128)}, f32[768,768]{1,0:T(8,128)}), (f32[768,2304]{1,0:T(8,128)}, f32[768,768]{1,0:T(8,128)})) %all-reduce.4.cloned.1.call-update) | async-done | bytes 9437200 | tf_op jit(solution)/shard_map/psum | solution.py:259
  572.5 6.6 %copy.111 = f32[768,2304]{1,0:T(8,128)} copy(f32[768,2304]{1,0:T(8,128)} %get-tuple-element.49) | data formatting | bytes 14155776
  (162 shorter events, 29.2 us)
Async XLA Ops:
  8.0 5.1 copy-start
  9.5 3.6 copy-start.32
  11.6 1.5 copy-start.35
  13.1 2.0 copy-start.18
  15.1 1.4 copy-start.25
  15.2 12.4 %copy-start.51 = (s32[4,128]{1,0:T(4,128)S(1)}, s32[4,128]{1,0:T(4,128)}, u32[]{:S(2)}) copy-start(s32[4,128]{1,0:T(4,128)} %param.15) | copy-start | bytes 6148
  17.8 15.9 %copy-start.52 = (s32[4,8]{1,0:T(4,128)S(1)}, s32[4,8]{1,0:T(4,128)}, u32[]{:S(2)}) copy-start(s32[4,8]{1,0:T(4,128)} %param.17) | copy-start | bytes 388
  17.8 37.0 %collective-permute-start.1 = (bf16[4,128,1536]{2,1,0:T(8,128)(2,1)}, bf16[4,128,1536]{2,1,0:T(8,128)(2,1)}, u32[]{:S(2)}, u32[]{:S(2)}) collective-permute-start(bf16[4,128,1536]{2,1,0:T(8,128)(2,1)} %slice.54), channel_id=1, source_target_pairs={{0,1},{1,2},{2,3},{3,4},{4,5},{5,6},{6,7},{8,9},{9,10},{10,11},{11... | collective-permute-start | bytes 4718600 | tf_op jit(solution)/shard_map/ppermute | solution.py:17
  22.9 51.4 %collective-permute-start = (bf16[4,128,1536]{2,1,0:T(8,128)(2,1)}, bf16[4,128,1536]{2,1,0:T(8,128)(2,1)}, u32[]{:S(2)}, u32[]{:S(2)}) collective-permute-start(bf16[4,128,1536]{2,1,0:T(8,128)(2,1)} %slice.54), channel_id=1, source_target_pairs={{0,2},{1,3},{2,4},{3,5},{4,6},{5,7},{8,10},{9,11},{10,12},{11,13},... | collective-permute-start | bytes 4718600 | tf_op jit(solution)/shard_map/ppermute | solution.py:17
  91.6 4.0 copy-start.1
  91.6 4.0 copy-start.30
  91.7 4.0 copy-start.11
  94.1 5.0 copy-start.31
  95.7 3.5 copy-start.5
  95.7 3.5 copy-start.27
  99.2 1.3 copy-start.22
  99.2 1.3 copy-start.42
  99.2 1.3 copy-start.47
  100.1 2.9 copy-start.7
  100.1 0.7 copy-start.46
  103.0 25.7 %all-to-all-start = ((bf16[16,64,768]{2,1,0:T(8,128)(2,1)}), bf16[16,64,768]{2,1,0:T(8,128)(2,1)}, u32[]{:S(2)}, u32[]{:S(2)}) async-start(bf16[16,64,768]{2,1,0:T(8,128)(2,1)} %bitcast.137), calls=%async_computation | async-start | bytes 3145728 | tf_op jit(solution)/shard_map/all_to_all | solution.py:149
  111.0 89.8 %copy-start.37 = (f32[4,128]{1,0:T(4,128)}, f32[4,128]{1,0:T(4,128)S(1)}, u32[]{:S(2)}) copy-start(f32[4,128]{1,0:T(4,128)S(1)} %convert_element_type.103) | copy-start | bytes 6148
  128.7 20.6 %all-to-all-start.2 = ((bf16[16,64,768]{2,1,0:T(8,128)(2,1)}), bf16[16,64,768]{2,1,0:T(8,128)(2,1)}, u32[]{:S(2)}, u32[]{:S(2)}) async-start(bf16[16,64,768]{2,1,0:T(8,128)(2,1)} %bitcast.135), calls=%async_computation.2 | async-start | bytes 3145728 | tf_op jit(solution)/shard_map/all_to_all | solution.py:174
  164.7 10.8 %copy-start.53 = (bf16[1024,3072]{1,0:T(8,128)(2,1)}, bf16[1024,3072]{1,0:T(8,128)(2,1)S(1)}, u32[]{:S(2)}) copy-start(bf16[1024,3072]{1,0:T(8,128)(2,1)S(1)} %fusion.6) | copy-start | bytes 18874372
  175.5 20.6 %all-to-all-start.3 = ((bf16[16,64,768]{2,1,0:T(8,128)(2,1)}), bf16[16,64,768]{2,1,0:T(8,128)(2,1)}, u32[]{:S(2)}, u32[]{:S(2)}) async-start(bf16[16,64,768]{2,1,0:T(8,128)(2,1)} %bitcast.136), calls=%async_computation.3 | async-start | bytes 3145728 | tf_op jit(solution)/shard_map/all_to_all | solution.py:189
  179.9 392.6 %all-reduce.4.cloned.1.call-start = ((), (), s32[]{:S(2)}) async-start(), calls=%async_computation.9 | async-start | bytes 18874368 | tf_op jit(solution)/shard_map/psum | solution.py:259
  196.1 4.0 copy-start.8
  196.1 4.0 copy-start.43
  200.1 1.8 copy-start.14
  200.7 1.2 copy-start.9
  200.7 2.4 copy-start.28
  200.8 1.4 copy-start.39
  202.2 0.9 copy-start.24
  209.5 8.0 %copy-start.12 = (bf16[4,384,768]{1,2,0:T(8,128)(2,1)S(1)}, bf16[4,384,768]{1,2,0:T(8,128)(2,1)}, u32[]{:S(2)}) copy-start(bf16[4,384,768]{1,2,0:T(8,128)(2,1)} %copy.77) | copy-start | bytes 7077892
  209.5 8.0 %copy-start.13 = (bf16[4,128,12,64]{1,0,3,2:T(4,128)(2,1)S(1)}, bf16[4,128,12,64]{1,0,3,2:T(4,128)(2,1)}, u32[]{:S(2)}) copy-start(bf16[4,128,12,64]{1,0,3,2:T(4,128)(2,1)} %reshape.347) | copy-start | bytes 2359300
  209.5 8.0 %copy-start.29 = (f32[4,12,128]{2,1,0:T(8,128)S(1)}, f32[4,12,128]{2,1,0:T(8,128)}, u32[]{:S(2)}) copy-start(f32[4,12,128]{2,1,0:T(8,128)} %log_add_fusion) | copy-start | bytes 73732
  232.0 7.5 %copy-start.10 = (bf16[4,128,768]{1,2,0:T(8,128)(2,1)S(1)}, bf16[4,128,768]{1,2,0:T(8,128)(2,1)}, u32[]{:S(2)}) copy-start(bf16[4,128,768]{1,2,0:T(8,128)(2,1)} %copy.78) | copy-start | bytes 2359300
  239.5 3.6 copy-start.2
  249.1 9.9 %copy-start.23 = (bf16[4,12,64,128]{3,2,1,0:T(8,128)(2,1)S(1)}, bf16[4,12,64,128]{3,2,1,0:T(8,128)(2,1)}, u32[]{:S(2)}) copy-start(bf16[4,12,64,128]{3,2,1,0:T(8,128)(2,1)} %copy-done.22) | copy-start | bytes 2359300
  249.1 11.4 %copy-start.3 = (bf16[4,12,128,384]{3,2,1,0:T(8,128)(2,1)S(1)}, bf16[4,12,128,384]{3,2,1,0:T(8,128)(2,1)}, u32[]{:S(2)}) copy-start(bf16[4,12,128,384]{3,2,1,0:T(8,128)(2,1)} %copy-done.2) | copy-start | bytes 14155780
  249.1 11.4 %copy-start.4 = (bf16[4,384,768]{1,2,0:T(8,128)(2,1)S(1)}, bf16[4,384,768]{1,2,0:T(8,128)(2,1)}, u32[]{:S(2)}) copy-start(bf16[4,384,768]{1,2,0:T(8,128)(2,1)} %copy.79) | copy-start | bytes 7077892
  255.6 72.1 %collective-permute-start.2 = (f32[4,128,1536]{2,1,0:T(8,128)}, f32[4,128,1536]{2,1,0:T(8,128)}, u32[]{:S(2)}, u32[]{:S(2)}) collective-permute-start(f32[4,128,1536]{2,1,0:T(8,128)} %get-tuple-element.32), channel_id=1, source_target_pairs={{2,0},{3,1},{4,2},{5,3},{6,4},{7,5},{10,8},{11,9},{12,10},{13,11},... | collective-permute-start | bytes 9437192 | tf_op jit(solution)/shard_map/ppermute | solution.py:17
  256.9 93.9 %collective-permute-start.3 = (f32[4,128,1536]{2,1,0:T(8,128)}, f32[4,128,1536]{2,1,0:T(8,128)}, u32[]{:S(2)}, u32[]{:S(2)}) collective-permute-start(f32[4,128,1536]{2,1,0:T(8,128)} %get-tuple-element.33), channel_id=1, source_target_pairs={{1,0},{2,1},{3,2},{4,3},{5,4},{6,5},{7,6},{9,8},{10,9},{11,10},{12... | collective-permute-start | bytes 9437192 | tf_op jit(solution)/shard_map/ppermute | solution.py:17
  269.5 86.9 %copy-start.19 = (bf16[4,128,768]{2,1,0:T(8,128)(2,1)S(1)}, bf16[4,128,768]{2,1,0:T(8,128)(2,1)}, u32[]{:S(2)}) copy-start(bf16[4,128,768]{2,1,0:T(8,128)(2,1)} %copy-done.18) | copy-start | bytes 2359300
  269.5 86.9 %copy-start.20 = (bf16[4,128,768]{2,1,0:T(8,128)(2,1)S(1)}, bf16[4,128,768]{2,1,0:T(8,128)(2,1)}, u32[]{:S(2)}) copy-start(bf16[4,128,768]{2,1,0:T(8,128)(2,1)} %copy.87) | copy-start | bytes 2359300
  355.3 1.1 copy-start.15
  361.5 211.1 %reduce-scatter.5.cloned.1.call-start = ((), (), s32[]{:S(2)}) async-start(), calls=%async_computation.8 | async-start | bytes 10616832 | tf_op jit(solution)/shard_map/reduce_scatter | solution.py:257
  374.4 198.2 %reduce-scatter.3.cloned.1.call-start = ((), (), s32[]{:S(2)}) async-start(), calls=%async_computation.7 | async-start | bytes 10616832 | tf_op jit(solution)/shard_map/reduce_scatter | solution.py:256
  385.8 16.6 %all-to-all-start.4 = ((s32[16,1,1]{2,1,0:T(1,128)}), s32[16,1,1]{2,1,0:T(1,128)S(1)}, u32[]{:S(2)}, u32[]{:S(2)}) async-start(s32[16,1,1]{2,1,0:T(1,128)} %copy.90), calls=%async_computation.6 | async-start | bytes 16384 | tf_op jit(solution)/shard_map/all_to_all | solution.py:146
  402.4 9.0 %copy-start.49 = (f32[768]{0:T(1024)S(1)}, f32[768]{0:T(1024)}, u32[]{:S(2)}) copy-start(f32[768]{0:T(1024)} %get-tuple-element.12) | copy-start | bytes 9220
  402.4 9.6 %copy-start.48 = (f32[768]{0:T(1024)S(1)}, f32[768]{0:T(1024)}, u32[]{:S(2)}) copy-start(f32[768]{0:T(1024)} %get-tuple-element.17) | copy-start | bytes 9220
  402.4 23.8 %all-to-all-start.1 = ((bf16[16,64,768]{2,1,0:T(8,128)(2,1)}), bf16[16,64,768]{2,1,0:T(8,128)(2,1)}, u32[]{:S(2)}, u32[]{:S(2)}) async-start(bf16[16,64,768]{2,1,0:T(8,128)(2,1)} %bitcast.134), calls=%async_computation.1 | async-start | bytes 3145728 | tf_op jit(solution)/shard_map/all_to_all | solution.py:155
  426.3 4.1 copy-start.6
  426.3 4.1 copy-start.16
  426.3 4.1 copy-start.21
  426.3 4.1 copy-start.33
  426.3 4.1 copy-start.34
  430.4 2.2 copy-start.41
  430.4 2.2 copy-start.36
  432.6 1.5 copy-start.17
  432.6 1.5 copy-start.44
  432.6 1.5 copy-start.45
  432.6 1.5 copy-start.38
  572.5 6.6 %copy-start.26 = (f32[768,768]{1,0:T(8,128)S(1)}, f32[768,768]{1,0:T(8,128)}, u32[]{:S(2)}) copy-start(f32[768,768]{1,0:T(8,128)} %get-tuple-element.50) | copy-start | bytes 7077892
  (2 other events, 1.2 us)
Sparse Core Ops, SparseCore 0:
  361.6 210.9 all-reduce.3
Sparse Core Ops, SparseCore 1:
  374.4 62.8 reduce-scatter.4
  440.1 59.7 reduce-scatter.2
where the time goes:
time: 598 us; the launch traced here: 588 us
  waiting for transfers between devices  213 us (36%)
  matrix products  131 us (22%)
  blocking collectives  76.4 us (13%)
  local copies, waits for them, and re-layouts  60.5 us (10%)
  other arithmetic  50.2 us (8%)
  starting transfers between devices  40.1 us (7%)
  between operations  17.3 us (3%)
    ppermute x4, waiting for transfers between devices, from_behind(): return lax.ppermute(block, axis, route)  112 us
    psum x1, blocking collectives, local(): lax.psum((qkv_local, proj_local, norm_terms, count_terms), ('batch', 'seq'))  76.4 us
    psum x1, waiting for transfers between devices, local(): lax.psum((qkv_local, proj_local, norm_terms, count_terms), ('batch', 'seq'))  55 us
    dot_general x6, matrix products, inner_rows(): lax.dot_general(left_side, right_side, (((0,), (0,)), ((), ())), preferre...  39.6 us
    dot_general x4, matrix products, times_transposed(): lax.dot_general(left_side, right_side, (((1,), (1,)), ((), ())), preferre...  29.9 us
    unnamed x110, local copies, waits for them, and re-layouts  15.4 us
    all_to_all x1, waiting for transfers between devices, local(): lax.all_to_all(result.reshape(owners, item_count, model_width), 'batch',...  13.7 us
    all_to_all x1, waiting for transfers between devices, local(): lax.all_to_all(outgoing, 'batch', split_axis=0, concat_axis=0, tiled=True)  13.5 us
  transfers between devices with their start and end apart: 12, of which 9 were waited for; matrix products, arithmetic and copies ran while one was open for 17% of the time, Pallas kernels for 0%

commit v1 on v0

v1 whole, which is shorter than its diff:
```python
import jax
import jax.numpy as jnp
from jax import lax
from jax.experimental import pallas as pl
from jax.experimental.pallas import tpu as pltpu
from jax.sharding import PartitionSpec as P

BF = jnp.bfloat16
F32 = jnp.float32
I32 = jnp.int32
EPS = 1e-05
MASKED = -1e30
HEADS = 12
HEAD_SIZE = 64
PAIRS = 6
CAP = 64
SWAP = [(i, i ^ 1) for i in range(8)]
UP_ONE = [(i, i + 1) for i in range(0, 8, 2)]
DOWN_ONE = [(i + 1, i) for i in range(0, 8, 2)]
AHEAD_TWO = [(i, i + 2) for i in range(6)]
BACK_TWO = [(i + 2, i) for i in range(6)]
PAY_ROWS = 10240
GEMM_ROWS = 9216
VM = pl.BlockSpec(memory_space=pltpu.VMEM)
SM = pl.BlockSpec(memory_space=pltpu.SMEM)


def shape(dims, kind=BF):
    return jax.ShapeDtypeStruct(dims, kind)


def kernel_call(body, outs, args, name, flops, grid=None, in_specs=None, out_specs=None, scratch=()):
    moved = sum(a.size * a.dtype.itemsize for a in args) + sum(
        o.size * o.dtype.itemsize for o in outs
    )
    extra = {} if grid is None else {"grid": grid}
    return pl.pallas_call(
        body,
        out_shape=outs,
        in_specs=in_specs or [VM] * len(args),
        out_specs=out_specs or [VM] * len(outs),
        scratch_shapes=list(scratch),
        compiler_params=pltpu.CompilerParams(vmem_limit_bytes=56 * 1024 * 1024),
        cost_estimate=pl.CostEstimate(flops=flops, bytes_accessed=moved, transcendentals=0),
        name=name,
        **extra,
    )(*args)


def nn(a, b):
    return jnp.dot(a, b, preferred_element_type=F32)


def nt(a, b):
    return lax.dot_general(a, b, (((1,), (1,)), ((), ())), preferred_element_type=F32)


def tn(a, b):
    return lax.dot_general(a, b, (((0,), (0,)), ((), ())), preferred_element_type=F32)


def iota(dims, axis):
    return lax.broadcasted_iota(I32, dims, axis)


def norm_parts(values):
    centred = values - jnp.mean(values, axis=-1, keepdims=True)
    inverse = lax.rsqrt(jnp.mean(centred * centred, axis=-1, keepdims=True) + EPS)
    return centred * inverse, inverse


def norm_back(grad, gain, unit, inverse):
    t = grad * gain
    return inverse * (
        t - jnp.mean(t, axis=-1, keepdims=True) - unit * jnp.mean(t * unit, axis=-1, keepdims=True)
    )


def route_kernel(tok, table, turn, grad, target_out, count_out, sent):
    ids = jnp.concatenate([tok[i : i + 1, :] for i in range(4)], axis=1)
    live = jnp.concatenate([turn[i : i + 1, :] for i in range(4)], axis=1).astype(F32)
    high, low = ids >> 7, ids & 127
    picked = nn(table[...], (iota((64, 512), 0) == high).astype(F32).astype(BF))
    chosen = jnp.sum(jnp.where(iota((128, 512), 0) == low, picked, 0.0), axis=0, keepdims=True)
    member = (iota((16, 512), 0) == chosen.astype(I32)).astype(F32)
    earlier = (iota((512, 512), 0) < iota((512, 512), 1)).astype(F32).astype(BF)
    before = nn(member.astype(BF), earlier)
    slot = jnp.sum(before * member, axis=0, keepdims=True)
    target = (chosen * CAP + slot).astype(I32)
    target_out[...] = jnp.broadcast_to(target, (8, 512))
    count_out[...] = jnp.broadcast_to(jnp.sum(member, axis=1, keepdims=True), (16, 128))
    for i in range(4):
        placing = jnp.where(iota((256, 512), 0) + 256 * i == target, live, 0.0).astype(BF)
        sent[256 * i : 256 * (i + 1), :] = nn(placing, grad[...]).astype(BF)


def own_kernel(x, gain, bias, weight, normed, query, keyval):
    unit, _ = norm_parts(x[...].astype(F32))
    rows = (unit * gain[...] + bias[...]).astype(BF)
    normed[...] = rows
    query[...] = nn(rows, weight[:, :768]).astype(BF)
    keyval[...] = nn(rows, weight[:, 768:]).astype(BF)


def head_masks(scale):
    lane = iota((1, 128), 1)
    first = jnp.where(lane < 64, scale, 0.0).astype(BF)
    second = jnp.where(lane >= 64, scale, 0.0).astype(BF)
    return first, second


def stack_heads(pair, masks):
    return jnp.concatenate([pair * masks[0], pair * masks[1]], axis=0)


def window_bias(start):
    key = iota((384, 128), 0)
    allowed = (key >= start) & (key <= iota((384, 128), 1) + 256)
    half = jnp.where(allowed, 0.0, MASKED)
    return jnp.concatenate([half, half], axis=1)


def join_heads(both):
    one = jnp.where(iota((128, 128), 0) < 64, both[:, :128], both[:, 128:])
    return one.T


def forward_kernel(
    behind_two, early, late, x, start, gain, bias, weight, query, keyval, proj, gain_two, bias_two,
    target, normed_halo, keyval_halo, attended, log_out, after_out, sent, context,
):
    scales = head_masks(HEAD_SIZE ** (-0.5))

    def one_row(r, carry):
        halo = jnp.concatenate([behind_two[r], early[r] + late[r]], axis=0).astype(F32)
        unit, _ = norm_parts(halo)
        rows = (unit * gain[...] + bias[...]).astype(BF)
        normed_halo[r] = rows
        fresh = nn(rows, weight[:, 768:]).astype(BF)
        keyval_halo[r] = fresh
        context[0:256, :] = fresh
        context[256:384, :] = keyval[r]
        mask = window_bias(start[r])
        for p in range(PAIRS):
            lo, hi = 128 * p, 128 * (p + 1)
            keys = context[:, lo:hi]
            values = context[:, 768 + lo : 768 + hi]
            stacked = stack_heads(query[r, :, lo:hi], scales)
            scores = nt(keys, stacked) + mask
            top = jnp.max(scores, axis=0, keepdims=True)
            weights = jnp.exp(scores - top)
            total = jnp.sum(weights, axis=0, keepdims=True)
            log_out[r, p : p + 1, :] = top + jnp.log(total)
            share = (weights * (1.0 / total)).astype(BF)
            attended[r, :, lo:hi] = join_heads(tn(values, share)).astype(BF)
        return carry

    lax.fori_loop(0, 4, one_row, 0)
    mixed = nn(attended[...].reshape(512, 768), proj[...])
    after = x[...].reshape(512, 768).astype(F32) + mixed
    after_out[...] = after
    unit, _ = norm_parts(after)
    rows = (unit * gain_two[...] + bias_two[...]).astype(BF)
    for i in range(4):
        placing = (iota((256, 512), 0) + 256 * i == target[0:1, :]).astype(F32).astype(BF)
        sent[256 * i : 256 * (i + 1), :] = nn(placing, rows).astype(BF)


def active_grad_kernel(grad, down, out):
    out[...] = nt(grad[...], down[...]).astype(BF)


def gelu_both(v):
    c = 0.7978845608028654
    square = v * v
    t = jnp.tanh(v * (c + (c * 0.044715) * square))
    half = 0.5 * v
    value = half + half * t
    slope = 0.5 + 0.5 * t + half * (1.0 - t * t) * (c + (3.0 * c * 0.044715) * square)
    return value, slope


def expert_kernel(x, up, raw, active, hidden_grad, back, total):
    step = pl.program_id(0)

    @pl.when(step == 0)
    def _():
        total[...] = jnp.zeros_like(total)

    for r in range(4):
        rows = slice(256 * r, 256 * (r + 1))
        value, slope = gelu_both(nn(x[rows, :], up[...]))
        active[rows, :] = value.astype(BF)
        low = (raw[rows, :].astype(F32) * slope).astype(BF)
        hidden_grad[rows, :] = low
        total[rows, :] += nt(low, up[...])

    @pl.when(step == pl.num_programs(0) - 1)
    def _():
        back[...] = total[...].astype(BF)


def weight_kernel(x, grad, active, hidden_grad, down, out, up_part, down_part, x_t, grad_t, total):
    step = pl.program_id(0)

    @pl.when(step == 0)
    def _():
        total[...] = jnp.zeros_like(total)
        x_t[...] = x[...].T
        grad_t[...] = grad[...].T

    total[...] += nn(active[...], down[...])
    one = nn(x_t[...], hidden_grad[...]).astype(BF)
    up_part[0] = one[:, :384]
    up_part[1] = one[:, 384:]
    two = nn(grad_t[...], active[...]).astype(BF)
    down_part[0] = two[:, :384]
    down_part[1] = two[:, 384:]

    @pl.when(step == pl.num_programs(0) - 1)
    def _():
        out[...] = total[...].astype(BF)


def output_kernel(after, target, returned, out):
    placing = (iota((512, 1024), 1) == target[...]).astype(F32).astype(BF)
    out[...] = (after[...] + nn(placing, returned[...])).astype(BF)


def middle_kernel(
    back, target, after, grad, turn, gain, proj, attended, after_grad, attended_grad, proj_part, terms
):
    placing = (iota((512, 1024), 1) == target[...]).astype(F32).astype(BF)
    normed_grad = nn(placing, back[...])
    unit, inverse = norm_parts(after[...])
    terms[0:1, :] = jnp.sum(normed_grad * unit, axis=0, keepdims=True)
    terms[1:2, :] = jnp.sum(normed_grad, axis=0, keepdims=True)
    upstream = grad[...].astype(F32) * turn[...]
    total = upstream + norm_back(normed_grad, gain[...], unit, inverse)
    after_grad[...] = total
    low = total.astype(BF)
    attended_grad[...] = nt(low, proj[...]).astype(BF)
    for i in range(3):
        proj_part[i] = tn(attended[...], low[:, 256 * i : 256 * (i + 1)]).astype(BF)


def backward_kernel(
    query, keyval, keyval_halo, attended_grad, log_total, start,
    query_grad, own_grad, halo_grad, context,
):
    scales = head_masks(HEAD_SIZE ** (-0.5))
    ones = head_masks(1.0)

    def one_row(r, carry):
        context[0:256, :] = keyval_halo[r]
        context[256:384, :] = keyval[r]
        mask = window_bias(start[r])
        for p in range(PAIRS):
            lo, hi = 128 * p, 128 * (p + 1)
            keys = context[:, lo:hi]
            values = context[:, 768 + lo : 768 + hi]
            stacked = stack_heads(query[r, :, lo:hi], scales)
            grads = stack_heads(attended_grad[r, :, lo:hi], ones)
            scores = nt(keys, stacked) + mask
            share = jnp.exp(scores - log_total[r, p : p + 1, :])
            share_grad = nt(values, grads)
            row_sum = jnp.sum(share * share_grad, axis=0, keepdims=True)
            score_grad = (share * (share_grad - row_sum)).astype(BF)
            key_grad = nn(score_grad, stacked).astype(BF)
            value_grad = nn(share.astype(BF), grads).astype(BF)
            halo_grad[r, :, lo:hi] = key_grad[:256]
            own_grad[r, :, lo:hi] = key_grad[256:]
            halo_grad[r, :, 768 + lo : 768 + hi] = value_grad[:256]
            own_grad[r, :, 768 + lo : 768 + hi] = value_grad[256:]
            turned = join_heads(tn(keys, score_grad))
            query_grad[r, :, lo:hi] = (turned * HEAD_SIZE ** (-0.5)).astype(BF)
        return carry

    lax.fori_loop(0, 4, one_row, 0)


def qkv_grad_kernel(normed, normed_halo, query_grad, own_grad, halo_grad, out, own_t, halo_t):
    step = pl.program_id(0)

    @pl.when(step == 0)
    def _():
        own_t[...] = normed[...].T
        halo_t[...] = normed_halo[...].T

    @pl.when(step < 3)
    def _():
        out[0] = nn(own_t[...], query_grad[...]).astype(BF)

    @pl.when(step >= 3)
    def _():
        out[0] = (nn(own_t[...], own_grad[...]) + nn(halo_t[...], halo_grad[...])).astype(BF)


def input_part_kernel(
    query_grad, own_grad, halo_grad, weight, x, behind_two, early, late, own_out, two_out, one_out, terms
):
    own = nt(query_grad[...], weight[:, :768]) + nt(own_grad[...], weight[:, 768:])
    own_out[...] = own
    unit, _ = norm_parts(x[...].astype(F32))
    gain_sum = jnp.sum(own * unit, axis=0, keepdims=True)
    bias_sum = jnp.sum(own, axis=0, keepdims=True)
    for r in range(4):
        part = nt(halo_grad[r], weight[:, 768:])
        two_out[r] = part[:128].astype(BF)
        one_out[r] = part[128:].astype(BF)
        halo = jnp.concatenate([behind_two[r], early[r] + late[r]], axis=0).astype(F32)
        unit, _ = norm_parts(halo)
        gain_sum += jnp.sum(part * unit, axis=0, keepdims=True)
        bias_sum += jnp.sum(part, axis=0, keepdims=True)
    terms[0:1, :] = gain_sum
    terms[1:2, :] = bias_sum


def input_grad_kernel(even, x, gain, own, from_one, from_two, after_grad, out):
    unit, inverse = norm_parts(x[...].astype(F32))
    total = own[...] + from_two[...].astype(F32) + even[0, 0] * from_one[...].astype(F32)
    out[...] = after_grad[...] + norm_back(total, gain[...], unit, inverse)


def along_x(d):
    return [(b, (b & 12) | ((b + d) & 3)) for b in range(16)]


def along_y(d):
    return [(b, (b + 4 * d) & 15) for b in range(16)]


def along_z(d):
    return [(s, (s + 2 * d) & 7) for s in range(8)]


def pick(array, index):
    return lax.dynamic_index_in_dim(array, index, 0, keepdims=False)


def meet(pieces, axis, route):
    got = [lax.ppermute(pieces[d], axis, route(d)) for d in (2, 1, 3)]
    total = pieces[0].astype(F32)
    for piece in got:
        total = total + piece.astype(F32)
    return total.astype(BF)


def gather(piece, axis, route, place):
    parts = [piece] + [lax.ppermute(piece, axis, route(d)) for d in (1, 2, 3)]
    stack = jnp.stack(parts)
    return jnp.stack([pick(stack, (place - p) % 4) for p in range(4)])


def sum_everywhere(payload):
    rows, lanes = payload.shape
    place = lax.axis_index("batch")
    x, y = place % 4, place // 4
    core = lax.axis_index("seq") % 2
    halves = payload.reshape(2, rows // 2, lanes)
    got = lax.ppermute(pick(halves, 1 - core), "seq", SWAP)
    dims = (2, 4, 4, rows // 64, lanes)
    kept, got = pick(halves, core).reshape(dims), got.reshape(dims)

    def parts(half, at):
        return [
            (pick(kept[half], (at + d) % 4).astype(F32) + pick(got[half], (at + d) % 4).astype(F32)).astype(BF)
            for d in range(4)
        ]

    one = meet(parts(0, x), "batch", along_x)
    two = meet(parts(1, y), "batch", along_y)
    one = meet([pick(one, (y + d) % 4) for d in range(4)], "batch", along_y)
    two = meet([pick(two, (x + d) % 4) for d in range(4)], "batch", along_x)
    both = meet([jnp.stack([one, two])] * 4, "seq", along_z)
    one = gather(both[0], "batch", along_y, y)
    two = gather(both[1], "batch", along_x, x)
    one = gather(one, "batch", along_x, x)
    two = gather(two, "batch", along_y, y)
    mine = jnp.stack([one, two]).reshape(rows // 2, lanes)
    other = lax.ppermute(mine, "seq", SWAP)
    joined = jnp.where(core == 0, jnp.stack([mine, other]), jnp.stack([other, mine]))
    return joined.reshape(rows, lanes)


def exchange(array):
    return lax.all_to_all(
        array.reshape(16, CAP, 768), "batch", split_axis=0, concat_axis=0, tiled=True
    ).reshape(1024, 768)


def local(
    block_input, token_ids, hash_table, doc_lengths, turn_mask, attn_norm_gain, attn_norm_bias,
    qkv_weight, proj_weight, ffn_norm_gain, ffn_norm_bias, expert_up, expert_down, out_grad,
):
    seq = lax.axis_index("seq")
    owner = lax.axis_index("batch")
    odd = seq % 2
    flat = (512, 768)
    rows3 = (4, 128, 768)
    gain_one, bias_one = attn_norm_gain.reshape(1, 768), attn_norm_bias.reshape(1, 768)
    gain_two, bias_two = ffn_norm_gain.reshape(1, 768), ffn_norm_bias.reshape(1, 768)
    up, down = expert_up[0], expert_down[0]

    behind_two = lax.ppermute(block_input, "seq", AHEAD_TWO)
    early = lax.ppermute(block_input, "seq", UP_ONE)
    late = lax.ppermute(behind_two, "seq", DOWN_ONE)

    ends = jnp.cumsum(doc_lengths, axis=-1)
    position = seq * 128 + jnp.arange(128, dtype=I32)
    start = jnp.max(
        jnp.where(ends[:, None, :] <= position[None, :, None], ends[:, None, :], 0), axis=-1
    )
    start = (start - (seq - 2) * 128).astype(I32).reshape(4, 1, 128)
    table = jnp.pad(hash_table, (0, 8192 - 8008)).reshape(64, 128).T.astype(BF)
    turn = turn_mask.reshape(512, 1).astype(F32)

    target, counts, grad_sent = kernel_call(
        route_kernel,
        [shape((8, 512), I32), shape((16, 128), F32), shape((1024, 768))],
        [token_ids, table, turn_mask, out_grad.reshape(flat)],
        "route", 10**9,
    )
    target_col = target[0].reshape(512, 1)
    grad_rows = exchange(grad_sent)

    normed, query, keyval = kernel_call(
        own_kernel,
        [shape(flat), shape(flat), shape((512, 1536))],
        [block_input.reshape(flat), gain_one, bias_one, qkv_weight],
        "own", 18 * 10**8,
    )
    query, keyval = query.reshape(rows3), keyval.reshape(4, 128, 1536)

    normed_halo, keyval_halo, attended, log_total, after, rows_sent = kernel_call(
        forward_kernel,
        [
            shape((4, 256, 768)), shape((4, 256, 1536)), shape(rows3), shape((4, 8, 256), F32),
            shape(flat, F32), shape((1024, 768)),
        ],
        [
            behind_two, early, late, block_input, start, gain_one, bias_one, qkv_weight, query, keyval,
            proj_weight, gain_two, bias_two, target,
        ],
        "forward", 8 * 10**9,
        scratch=[pltpu.VMEM((384, 1536), BF)],
    )
    rows = exchange(rows_sent)

    raw = kernel_call(
        active_grad_kernel,
        [shape((1024, 3072))],
        [grad_rows, down],
        "active_grad", 48 * 10**8,
        grid=(6,),
        in_specs=[
            pl.BlockSpec((1024, 768), lambda i: (0, 0)),
            pl.BlockSpec((512, 768), lambda i: (i, 0)),
        ],
        out_specs=[pl.BlockSpec((1024, 512), lambda i: (0, i))],
    )[0]

    active, hidden_grad, back_sent = kernel_call(
        expert_kernel,
        [shape((1024, 3072)), shape((1024, 3072)), shape((1024, 768))],
        [rows, up, raw],
        "expert", 97 * 10**8,
        grid=(6,),
        in_specs=[
            pl.BlockSpec((1024, 768), lambda i: (0, 0)),
            pl.BlockSpec((768, 512), lambda i: (0, i)),
            pl.BlockSpec((1024, 512), lambda i: (0, i)),
        ],
        out_specs=[
            pl.BlockSpec((1024, 512), lambda i: (0, i)),
            pl.BlockSpec((1024, 512), lambda i: (0, i)),
            pl.BlockSpec((1024, 768), lambda i: (0, 0)),
        ],
        scratch=[pltpu.VMEM((1024, 768), F32)],
    )
    back = exchange(back_sent)

    result, up_part, down_part = kernel_call(
        weight_kernel,
        [shape((1024, 768)), shape((8, 768, 384)), shape((8, 768, 384))],
        [rows, grad_rows, active, hidden_grad, down],
        "weights", 145 * 10**8,
        grid=(4,),
        in_specs=[
            pl.BlockSpec((1024, 768), lambda i: (0, 0)),
            pl.BlockSpec((1024, 768), lambda i: (0, 0)),
            pl.BlockSpec((1024, 768), lambda i: (0, i)),
            pl.BlockSpec((1024, 768), lambda i: (0, i)),
            pl.BlockSpec((768, 768), lambda i: (i, 0)),
        ],
        out_specs=[
            pl.BlockSpec((1024, 768), lambda i: (0, 0)),
            pl.BlockSpec((2, 768, 384), lambda i: (i, 0, 0)),
            pl.BlockSpec((2, 768, 384), lambda i: (i, 0, 0)),
        ],
        scratch=[pltpu.VMEM((768, 1024), BF), pltpu.VMEM((768, 1024), BF), pltpu.VMEM((1024, 768), F32)],
    )
    returned = exchange(result)
    up_sum = lax.psum_scatter(up_part, "seq", scatter_dimension=0, tiled=True)
    down_sum = lax.psum_scatter(down_part, "seq", scatter_dimension=0, tiled=True)

    after_grad, attended_grad, proj_part, terms_two = kernel_call(
        middle_kernel,
        [shape(flat, F32), shape(flat), shape((3, 768, 256)), shape((2, 768), F32)],
        [back, target_col, after, out_grad.reshape(flat), turn, gain_two, proj_weight, attended.reshape(flat)],
        "middle", 2 * 10**9,
    )

    query_grad, own_grad, halo_grad = kernel_call(
        backward_kernel,
        [shape(rows3), shape((4, 128, 1536)), shape((4, 256, 1536))],
        [query, keyval, keyval_halo, attended_grad.reshape(rows3), log_total, start],
        "backward", 6 * 10**9,
        scratch=[pltpu.VMEM((384, 1536), BF)],
    )
    query_grad, own_grad = query_grad.reshape(flat), own_grad.reshape(512, 1536)

    qkv_part = kernel_call(
        qkv_grad_kernel,
        [shape((9, 768, 256))],
        [normed, normed_halo.reshape(1024, 768), query_grad, own_grad, halo_grad.reshape(1024, 1536)],
        "qkv_grad", 42 * 10**8,
        grid=(9,),
        in_specs=[
            pl.BlockSpec((512, 768), lambda i: (0, 0)),
            pl.BlockSpec((1024, 768), lambda i: (0, 0)),
            pl.BlockSpec((512, 256), lambda i: (0, jnp.minimum(i, 2))),
            pl.BlockSpec((512, 256), lambda i: (0, jnp.maximum(i - 3, 0))),
            pl.BlockSpec((1024, 256), lambda i: (0, jnp.maximum(i - 3, 0))),
        ],
        out_specs=[pl.BlockSpec((1, 768, 256), lambda i: (i, 0, 0))],
        scratch=[pltpu.VMEM((768, 512), BF), pltpu.VMEM((768, 1024), BF)],
    )[0]

    input_own, input_two, input_one, terms_one = kernel_call(
        input_part_kernel,
        [shape(flat, F32), shape(rows3), shape(rows3), shape((2, 768), F32)],
        [query_grad, own_grad, halo_grad, qkv_weight, block_input.reshape(flat), behind_two, early, late],
        "input_part", 42 * 10**8,
    )
    from_one = lax.ppermute(input_one, "seq", SWAP)
    passed = jnp.where(odd == 1, input_two + from_one, input_two)
    from_two = lax.ppermute(passed, "seq", BACK_TWO)
    even = (1 - odd).astype(F32).reshape(1, 1)
    input_grad = kernel_call(
        input_grad_kernel,
        [shape(flat, F32)],
        [
            even, block_input.reshape(flat), gain_one, input_own, from_one.reshape(flat),
            from_two.reshape(flat), after_grad,
        ],
        "input_grad", 10**7,
        in_specs=[SM] + [VM] * 6,
    )[0]

    here = jnp.arange(128, dtype=I32) == seq * 16 + owner
    tally = jnp.where(here[None, :], counts, 0.0).reshape(2048)
    extra = jnp.concatenate([terms_one.reshape(-1), terms_two.reshape(-1), tally]).astype(BF)
    extra = jnp.pad(extra, (0, (PAY_ROWS - GEMM_ROWS) * 256 - extra.size)).reshape(-1, 256)
    payload = jnp.concatenate([qkv_part.reshape(-1, 256), proj_part.reshape(-1, 256), extra], axis=0)
    summed = sum_everywhere(payload)
    blocks = summed[:GEMM_ROWS].reshape(12, 768, 256).astype(F32)
    qkv_sum = jnp.transpose(blocks[:9], (1, 0, 2)).reshape(768, 2304)
    proj_sum = jnp.transpose(blocks[9:], (1, 0, 2)).reshape(768, 768)
    tail = summed[GEMM_ROWS:].reshape(-1).astype(F32)
    terms = tail[:3072].reshape(4, 768)
    every = tail[3072:5120].reshape(16, 8, 16).astype(I32)

    block_output = kernel_call(
        output_kernel, [shape(flat)], [after, target_col, returned], "output", 8 * 10**8
    )[0]
    return (
        block_output.reshape(rows3),
        input_grad.reshape(rows3),
        terms[0],
        terms[1],
        qkv_sum,
        proj_sum,
        terms[2],
        terms[3],
        up_sum.astype(F32),
        jnp.swapaxes(down_sum.astype(F32), 1, 2),
        jnp.sum(every, axis=(1, 2)),
        lax.dynamic_slice(every, (owner, seq, 0), (1, 1, 16)),
    )


def solution(mesh):
    placed = (
        P("batch", "seq", None),
        P("batch", "seq"),
        P(),
        P("batch", None),
        P("batch", "seq"),
        P(),
        P(),
        P(),
        P(),
        P(),
        P(),
        P("batch", None, None),
        P("batch", None, None),
        P("batch", "seq", None),
    )
    return jax.shard_map(
        local,
        mesh=mesh,
        in_specs=placed,
        out_specs=(
            P("batch", "seq", None),
            P("batch", "seq", None),
            P(),
            P(),
            P(),
            P(),
            P(),
            P(),
            P("batch", None, "seq"),
            P("batch", "seq", None),
            P(),
            P("batch", "seq", None),
        ),
        check_vma=False,
    )
```

time: 598 us -> 417 us (0.70)
  Pallas kernels: 0 us -> 141 us
  matrix products: 131 us -> 0 us
  waiting for transfers between devices: 213 us -> 82.3 us
  blocking collectives: 76.4 us -> 0 us
  starting transfers between devices: 40.1 us -> 82.5 us
  other arithmetic: 50.2 us -> 38.5 us
  local copies, waits for them, and re-layouts: 60.5 us -> 49.6 us
    pallas_call x0 -> x12, Pallas kernels: none -> 141 us  [kernel_call(): pl.pallas_call(body, out_shape=outs, in_specs=in_specs or [VM] * len(args...]
    dot_general x22 -> x0, matrix products: 131 us -> none  [the longest x6 39.6 us: inner_rows(): lax.dot_general(left_side, right_side, (((0,), (0,)), ((), ())), preferre...]
    psum x1 -> x0, blocking collectives: 76.4 us -> none  [local(): lax.psum((qkv_local, proj_local, norm_terms, count_terms), ('batch', 'seq'))]
    ppermute x4 -> x34, waiting for transfers between devices: 112 us -> 45.8 us  [the longest x15 17.1 us: meet(): got = [lax.ppermute(pieces[d], axis, route(d)) for d in (2, 1, 3)]]
    psum x1 -> x0, waiting for transfers between devices: 55 us -> none  [local(): lax.psum((qkv_local, proj_local, norm_terms, count_terms), ('batch', 'seq'))]
    ppermute x4 -> x34, starting transfers between devices: 13.2 us -> 59.3 us  [the longest x15 24 us: meet(): got = [lax.ppermute(pieces[d], axis, route(d)) for d in (2, 1, 3)]]
    reshape x3 -> x7, local copies, waits for them, and re-layouts: 14.6 us -> 2.54 us  [the longest x1 0.58 us: local(): attn_norm_gain.reshape(1, 768)]
    transpose x0 -> x2, local copies, waits for them, and re-layouts: none -> 10 us  [the longest x1 7.98 us: local(): qkv_sum = jnp.transpose(blocks[:9], (1, 0, 2)).reshape(768, 2304)]
  transfers between devices with their start and end apart: 12 -> 40, of which waited for: 9 -> 18; matrix products, arithmetic and copies ran while one was open for 17% -> 19% of each run, Pallas kernels for 0% -> 29%
where the time goes in v1:
time: 417 us; the launch traced here: 409 us
  Pallas kernels  141 us (34%)
  starting transfers between devices  82.5 us (20%)
  waiting for transfers between devices  82.3 us (20%)
  local copies, waits for them, and re-layouts  49.6 us (12%)
  other arithmetic  38.5 us (9%)
  between operations  14.8 us (4%)
    pallas_call x12, Pallas kernels, kernel_call(): pl.pallas_call(body, out_shape=outs, in_specs=in_specs or [VM] * len(args...  141 us
    all_to_all x4, waiting for transfers between devices, exchange(): lax.all_to_all(array.reshape(16, CAP, 768), 'batch', split_axis=0, concat...  36.4 us
    ppermute x15, starting transfers between devices, meet(): got = [lax.ppermute(pieces[d], axis, route(d)) for d in (2, 1, 3)]  24 us
    all_to_all x4, starting transfers between devices, exchange(): lax.all_to_all(array.reshape(16, CAP, 768), 'batch', split_axis=0, concat...  23 us
    unnamed x39, local copies, waits for them, and re-layouts  21.7 us
    ppermute x15, waiting for transfers between devices, meet(): got = [lax.ppermute(pieces[d], axis, route(d)) for d in (2, 1, 3)]  17.1 us
    concatenate x1, other arithmetic, local(): jnp.concatenate([qkv_part.reshape(-1, 256), proj_part.reshape(-1, 256), e...  16.9 us
    ppermute x12, starting transfers between devices, gather(): parts = [piece] + [lax.ppermute(piece, axis, route(d)) for d in (1, 2, 3)]  14.2 us
  transfers between devices with their start and end apart: 40, of which 18 were waited for; matrix products, arithmetic and copies ran while one was open for 19% of the time, Pallas kernels for 29%

profile of v1, /device:TPU:1, one launch (start us, length us, event | category | flops | bytes accessed | tf_op | source)
XLA Modules:
  0.0 408.7 jit_solution(5566412669163147227)
XLA Ops:
  7.2 4.4 %collective-permute-start = (bf16[4,128,768]{2,1,0:T(8,128)(2,1)}, bf16[4,128,768]{2,1,0:T(8,128)(2,1)S(1)}, u32[]{:S(2)}, u32[]{:S(2)}) collective-permute-start(bf16[4,128,768]{2,1,0:T(8,128)(2,1)} %x.5), channel_id=1, source_target_pairs={{0,2},{1,3},{2,4},{3,5},{4,6},{5,7},{8,10},{9,11},{10,12},{11,13},... | collective-permute-start | bytes 2359304 | tf_op jit(solution)/shard_map/ppermute | solution.py:405
  11.6 1.3 collective-permute-start.1
  14.4 13.7 %collective-permute-done.behind_two = bf16[4,128,768]{2,1,0:T(8,128)(2,1)S(1)} collective-permute-done((bf16[4,128,768]{2,1,0:T(8,128)(2,1)}, bf16[4,128,768]{2,1,0:T(8,128)(2,1)S(1)}, u32[]{:S(2)}, u32[]{:S(2)}) %collective-permute-start) | collective-permute-done | bytes 786464 | tf_op jit(solution)/shard_map/ppermute | solution.py:405
  28.1 4.4 %collective-permute-start.2 = (bf16[4,128,768]{2,1,0:T(8,128)(2,1)S(1)}, bf16[4,128,768]{2,1,0:T(8,128)(2,1)}, u32[]{:S(2)}, u32[]{:S(2)}) collective-permute-start(bf16[4,128,768]{2,1,0:T(8,128)(2,1)S(1)} %collective-permute-done.behind_two), channel_id=1, source_target_pairs={{1,0},{3,2},{5,4},{7,6},{9,8},{11,10},{13,12},{15,14},{17,16},{19,... | collective-permute-start | bytes 2359304 | tf_op jit(solution)/shard_map/ppermute | solution.py:407
  32.4 3.6 route.1
  36.1 6.9 %all-to-all-start.1 = ((bf16[16,64,768]{2,1,0:T(8,128)(2,1)}), bf16[16,64,768]{2,1,0:T(8,128)(2,1)S(1)}, u32[]{:S(2)}, u32[]{:S(2)}) async-start(bf16[16,64,768]{2,1,0:T(8,128)(2,1)} %bitcast.152), calls=%async_computation.1 | async-start | bytes 3145728 | tf_op jit(solution)/shard_map/all_to_all | solution.py:387
  45.6 5.8 %own.1 = (bf16[512,768]{1,0:T(8,128)(2,1)}, bf16[512,768]{1,0:T(8,128)(2,1)}, bf16[512,1536]{1,0:T(8,128)(2,1)}) custom-call(bf16[512,768]{1,0:T(8,128)(2,1)} %bitcast.158, f32[1,768]{1,0:T(1,128)} %reshape.259.gain, f32[1,768]{1,0:T(1,128)} %reshape.260.bias, bf16[768,2304]{1,0:T(8,128)(2,1)} %weight.5), custom_call_target="tpu_custom_call" | custom-call | flops 1800000000 | bytes 7477248 | tf_op jit(solution)/shard_map/own/pallas_call | solution.py:37
  52.9 22.3 %forward.1 = (bf16[4,256,768]{2,1,0:T(8,128)(2,1)}, bf16[4,256,1536]{2,1,0:T(8,128)(2,1)}, bf16[4,128,768]{2,1,0:T(8,128)(2,1)}, f32[4,8,256]{2,1,0:T(8,128)}, f...) custom-call(bf16[4,128,768]{2,1,0:T(8,128)(2,1)} %copy-done.16, bf16[4,128,768]{2,1,0:T(8,128)(2,1)} %copy-done.17, ...), custom_call_target="tpu_custom_call" | custom-call | flops 8000000000 | bytes 18937856 | tf_op jit(solution)/shard_map/forward/pallas_call | solution.py:37
  76.4 7.2 %all-to-all-start = ((bf16[16,64,768]{2,1,0:T(8,128)(2,1)}), bf16[16,64,768]{2,1,0:T(8,128)(2,1)S(1)}, u32[]{:S(2)}, u32[]{:S(2)}) async-start(bf16[16,64,768]{2,1,0:T(8,128)(2,1)} %bitcast.151), calls=%async_computation | async-start | bytes 3145728 | tf_op jit(solution)/shard_map/all_to_all | solution.py:387
  86.0 9.8 %active_grad.1.raw = bf16[1024,3072]{1,0:T(8,128)(2,1)} custom-call(bf16[1024,768]{1,0:T(8,128)(2,1)} %bitcast.147, bf16[3072,768]{1,0:T(8,128)(2,1)} %bitcast.178), custom_call_target="tpu_custom_call" | custom-call | flops 4800000000 | bytes 12582912 | tf_op jit(solution)/shard_map/active_grad/pallas_call | solution.py:37
  95.9 14.4 %all-to-all-done = bf16[16,64,768]{2,1,0:T(8,128)(2,1)S(1)} async-done(((bf16[16,64,768]{2,1,0:T(8,128)(2,1)}), bf16[16,64,768]{2,1,0:T(8,128)(2,1)S(1)}, u32[]{:S(2)}, u32[]{:S(2)}) %all-to-all-start) | async-done | bytes 1572896 | tf_op jit(solution)/shard_map/all_to_all | solution.py:387
  111.4 22.1 %expert.1 = (bf16[1024,3072]{1,0:T(8,128)(2,1)}, bf16[1024,3072]{1,0:T(8,128)(2,1)}, bf16[1024,768]{1,0:T(8,128)(2,1)}) custom-call(bf16[1024,768]{1,0:T(8,128)(2,1)} %bitcast.149, bf16[768,3072]{1,0:T(8,128)(2,1)} %bitcast.177, bf16[1024,3072]{1,0:T(8,128)(2,1)} %active_grad.1.raw), custom_call_target="tpu_custom_call" | custom-call | flops 9699999744 | bytes 26738688 | tf_op jit(solution)/shard_map/expert/pallas_call | solution.py:37
  133.6 3.7 all-to-all-start.3
  137.3 22.3 %weights.1 = (bf16[1024,768]{1,0:T(8,128)(2,1)}, bf16[8,768,384]{2,1,0:T(8,128)(2,1)}, bf16[8,768,384]{2,1,0:T(8,128)(2,1)}) custom-call(bf16[1024,768]{1,0:T(8,128)(2,1)} %bitcast.150, bf16[1024,768]{1,0:T(8,128)(2,1)} %bitcast.148, bf16[1024,3072]{1,0:T(8,128)(2,1)} %get-tuple-element.47.active, bf16[1024,3072]{1,0:T(8,128)(2,1)} %get-tuple-element.48.hidden_grad, ...), custom_call_target="tpu_custom_call" | custom-call | flops 14499999744 | bytes 31457280 | tf_op jit(solution)/shard_map/weights/pallas_call | solution.py:37
  159.9 2.4 all-to-all-done.3
  163.4 7.4 %middle.1 = (f32[512,768]{1,0:T(8,128)}, bf16[512,768]{1,0:T(8,128)(2,1)}, bf16[3,768,256]{2,1,0:T(8,128)(2,1)}, f32[2,768]{1,0:T(2,128)}) custom-call(bf16[1024,768]{1,0:T(8,128)(2,1)} %bitcast.153, s32[512,1]{1,0:T(8,128)} %copy.46.target, f32[512,768]{1,0:T(8,128)} %get-tuple-element.44.after, bf16[512,768]{1,0:T(8,128)(2,1)} %bitcast.181, ...), custom_call_target="tpu_custom_call" | custom-call | flops 2000000000 | bytes 9450496 | tf_op jit(solution)/shard_map/middle/pallas_call | solution.py:37
  171.5 16.4 %backward.1 = (bf16[4,128,768]{2,1,0:T(8,128)(2,1)}, bf16[4,128,1536]{2,1,0:T(8,128)(2,1)}, bf16[4,256,1536]{2,1,0:T(8,128)(2,1)}) custom-call(bf16[4,128,768]{2,1,0:T(8,128)(2,1)} %bitcast.189, bf16[4,128,1536]{2,1,0:T(8,128)(2,1)} %bitcast.185, bf16[4,256,1536]{2,1,0:T(8,128)(2,1)} %get-tuple-element.50.keyval_halo, bf16[4,128,768]{2,1,0:T(8,128)(2,1)} %bitcast.193, ...), custom_call_target="tpu_custom_call" | custom-call | flops 6000000000 | bytes 11831296 | tf_op jit(solution)/shard_map/backward/pallas_call | solution.py:37
  187.9 10.8 %input_part.1 = (f32[512,768]{1,0:T(8,128)}, bf16[4,128,768]{2,1,0:T(8,128)(2,1)}, bf16[4,128,768]{2,1,0:T(8,128)(2,1)}, f32[2,768]{1,0:T(2,128)}) custom-call(bf16[512,768]{1,0:T(8,128)(2,1)} %bitcast.191, bf16[512,1536]{1,0:T(8,128)(2,1)} %bitcast.186, bf16[4,256,1536]{2,1,0:T(8,128)(2,1)} %get-tuple-element.57.halo_grad, bf16[768,2304]{1,0:T(8,128)(2,1)} %weight.5, ...), custom_call_target="tpu_custom_call" | custom-call | flops 4200000000 | bytes 15341568 | tf_op jit(solution)/shard_map/input_part/pallas_call | solution.py:37
  199.6 11.6 %qkv_grad.1 = bf16[9,768,256]{2,1,0:T(8,128)(2,1)} custom-call(bf16[512,768]{1,0:T(8,128)(2,1)} %get-tuple-element.62.normed, bf16[1024,768]{1,0:T(8,128)(2,1)} %bitcast.183, bf16[512,768]{1,0:T(8,128)(2,1)} %bitcast.192, bf16[512,1536]{1,0:T(8,128)(2,1)} %bitcast.187, bf16[1024,1536]{1,0:T(8,128)(2,1)} %bitcast.182), custom_call_target="tpu_custom_call" | custom-call | flops 4200000000 | bytes 11403264 | tf_op jit(solution)/shard_map/qkv_grad/pallas_call | solution.py:37
  211.2 16.9 %pad_maximum_fusion = bf16[10240,256]{1,0:T(8,128)(2,1)S(1)} fusion(bf16[1024,256]{1,0:T(8,128)(2,1)S(1)} %reshape.291, bf16[2304,256]{1,0:T(8,128)(2,1)S(1)} %bitcast.156, bf16[6912,256]{1,0:T(8,128)(2,1)} %bitcast.144), kind=kLoop, calls=%fused_computation | loop fusion | flops 15728640 | bytes 10485760 | tf_op jit(solution)/shard_map/concatenate | solution.py:565
  228.4 2.2 copy-done.2
  230.6 1.2 collective-permute-start.5
  231.8 2.9 constant_dynamic-slice_fusion.12
  234.7 1.7 collective-permute-done.5
  236.4 1.9 fusion.30
  239.4 1.6 collective-permute-start.14
  242.2 1.4 fusion.12
  243.6 1.4 collective-permute-start.8
  245.1 3.5 collective-permute-done.14
  248.6 7.4 %collective-permute-start.6 = (bf16[4,160,256]{2,1,0:T(8,128)(2,1)S(1)}, bf16[4,160,256]{2,1,0:T(8,128)(2,1)S(1)}, u32[]{:S(2)}, u32[]{:S(2)}) collective-permute-start(bf16[4,160,256]{2,1,0:T(8,128)(2,1)S(1)} %get-tuple-element.120), channel_id=1, source_target_pairs={{0,16},{8,24},{16,0},{24,8},{32,48},{40,56},{48,32},{56,40},{64,80... | collective-permute-start | bytes 983048 | tf_op jit(solution)/shard_map/ppermute | solution.py:342
  256.0 1.9 collective-permute-done.13
  257.9 1.5 fusion.5
  259.5 1.5 collective-permute-start.16
  261.6 1.2 fusion.8
  262.8 3.8 collective-permute-start.11
  266.7 1.3 collective-permute-start.9
  268.2 4.3 %collective-permute-done.10 = bf16[160,256]{1,0:T(8,128)(2,1)S(1)} collective-permute-done((bf16[160,256]{1,0:T(8,128)(2,1)S(1)}, bf16[160,256]{1,0:T(8,128)(2,1)S(1)}, u32[]{:S(2)}, u32[]{:S(2)}) %collective-permute-start.10) | collective-permute-done | bytes 81952 | tf_op jit(solution)/shard_map/ppermute | solution.py:342
  272.5 4.0 collective-permute-start.20
  276.6 1.5 collective-permute-start.18
  278.1 3.6 collective-permute-done.20
  281.6 3.3 collective-permute-done.19
  285.1 2.4 collective-permute-start.23
  288.1 2.9 collective-permute-start.29
  293.2 2.6 collective-permute-start.26
  297.1 2.3 collective-permute-start.32
  300.4 4.8 %collective-permute-done.26 = bf16[4,160,256]{2,1,0:T(8,128)(2,1)S(1)} collective-permute-done((bf16[4,160,256]{2,1,0:T(8,128)(2,1)S(1)}, bf16[4,160,256]{2,1,0:T(8,128)(2,1)S(1)}, u32[]{:S(2)}, u32[]{:S(2)}) %collective-permute-start.26) | collective-permute-done | bytes 327712 | tf_op jit(solution)/shard_map/ppermute | solution.py:350
  305.2 3.9 collective-permute-done.24
  309.4 3.2 collective-permute-done.30
  313.5 8.3 %collective-permute-start.33 = (bf16[5120,256]{1,0:T(8,128)(2,1)S(1)}, bf16[5120,256]{1,0:T(8,128)(2,1)}, u32[]{:S(2)}, u32[]{:S(2)}) collective-permute-start(bf16[5120,256]{1,0:T(8,128)(2,1)S(1)} %bitcast.133), channel_id=1, source_target_pairs={{0,1},{1,0},{2,3},{3,2},{4,5},{5,4},{6,7},{7,6},{8,9},{9,8},{10,11... | collective-permute-start | bytes 7864328 | tf_op jit(solution)/shard_map/ppermute | solution.py:381
  321.9 5.2 %all-to-all-start.2 = ((bf16[16,64,768]{2,1,0:T(8,128)(2,1)}), bf16[16,64,768]{2,1,0:T(8,128)(2,1)}, u32[]{:S(2)}, u32[]{:S(2)}) async-start(bf16[16,64,768]{2,1,0:T(8,128)(2,1)} %bitcast.146), calls=%async_computation.2 | async-start | bytes 3145728 | tf_op jit(solution)/shard_map/all_to_all | solution.py:387
  327.5 2.4 add_select_fusion
  329.9 1.5 collective-permute-start.4
  331.4 19.6 %all-to-all-done.2 = bf16[16,64,768]{2,1,0:T(8,128)(2,1)} async-done(((bf16[16,64,768]{2,1,0:T(8,128)(2,1)}), bf16[16,64,768]{2,1,0:T(8,128)(2,1)}, u32[]{:S(2)}, u32[]{:S(2)}) %all-to-all-start.2) | async-done | bytes 1572896 | tf_op jit(solution)/shard_map/all_to_all | solution.py:387
  350.9 4.0 output.1
  354.9 5.0 %input_grad.1 = f32[512,768]{1,0:T(8,128)} custom-call(f32[1,1]{1,0:T(1,128)} %bitcast.17.even, bf16[512,768]{1,0:T(8,128)(2,1)} %bitcast.160, f32[1,768]{1,0:T(1,128)} %reshape.259.gain, f32[512,768]{1,0:T(8,128)} %get-tuple-element.58.own, bf16[512,768]{1,0:T(8,128)(2,1)} %bitcast.145, bf16[512,768]{1,0:T(8,128)(2,1)} %bitcast.26.from_two, ...), custom_call_target="tpu_custom_call" | custom-call | flops 10000000 | bytes 7080964 | tf_op jit(solution)/shard_map/input_grad/pallas_call | solution.py:37
  359.9 3.9 maximum_select_fusion
  364.6 3.9 slice.128
  368.5 2.2 copy-done
  372.4 8.0 %copy.49 = f32[768,9,256]{0,2,1:T(8,128)} copy(f32[768,9,256]{2,0,1:T(8,128)} %bitcast.126) | data formatting | bytes 14155776 | tf_op jit(solution)/shard_map/transpose | solution.py:568
  380.4 8.1 %copy.51 = f32[768,2304]{1,0:T(8,128)} copy(f32[768,2304]{0,1:T(8,128)} %bitcast.127) | data formatting | bytes 14155776
  388.5 2.0 copy.50
  390.6 3.0 copy.52
  398.2 1.4 copy.53
  399.5 2.2 convert_element_type.297
  (139 shorter events, 30.9 us)
Async XLA Ops:
  7.2 20.9 %collective-permute-start = (bf16[4,128,768]{2,1,0:T(8,128)(2,1)}, bf16[4,128,768]{2,1,0:T(8,128)(2,1)S(1)}, u32[]{:S(2)}, u32[]{:S(2)}) collective-permute-start(bf16[4,128,768]{2,1,0:T(8,128)(2,1)} %x.5), channel_id=1, source_target_pairs={{0,2},{1,3},{2,4},{3,5},{4,6},{5,7},{8,10},{9,11},{10,12},{11,13},... | collective-permute-start | bytes 2359304 | tf_op jit(solution)/shard_map/ppermute | solution.py:405
  11.6 40.4 %collective-permute-start.1 = (bf16[4,128,768]{2,1,0:T(8,128)(2,1)}, bf16[4,128,768]{2,1,0:T(8,128)(2,1)S(1)}, u32[]{:S(2)}, u32[]{:S(2)}) collective-permute-start(bf16[4,128,768]{2,1,0:T(8,128)(2,1)} %x.5), channel_id=1, source_target_pairs={{0,1},{2,3},{4,5},{6,7},{8,9},{10,11},{12,13},{14,15},{16,17},{18,... | collective-permute-start | bytes 2359304 | tf_op jit(solution)/shard_map/ppermute | solution.py:406
  28.1 8.0 %copy-start.16 = (bf16[4,128,768]{2,1,0:T(8,128)(2,1)}, bf16[4,128,768]{2,1,0:T(8,128)(2,1)S(1)}, u32[]{:S(2)}) copy-start(bf16[4,128,768]{2,1,0:T(8,128)(2,1)S(1)} %collective-permute-done.behind_two) | copy-start | bytes 2359300
  28.1 24.0 %collective-permute-start.2 = (bf16[4,128,768]{2,1,0:T(8,128)(2,1)S(1)}, bf16[4,128,768]{2,1,0:T(8,128)(2,1)}, u32[]{:S(2)}, u32[]{:S(2)}) collective-permute-start(bf16[4,128,768]{2,1,0:T(8,128)(2,1)S(1)} %collective-permute-done.behind_two), channel_id=1, source_target_pairs={{1,0},{3,2},{5,4},{7,6},{9,8},{11,10},{13,12},{15,14},{17,16},{19,... | collective-permute-start | bytes 2359304 | tf_op jit(solution)/shard_map/ppermute | solution.py:407
  36.1 7.0 %copy-start.10 = (f32[768]{0:T(1024)S(1)}, f32[768]{0:T(1024)}, u32[]{:S(2)}) copy-start(f32[768]{0:T(1024)} %param.19) | copy-start | bytes 9220
  36.1 7.6 %copy-start.11 = (f32[768]{0:T(1024)S(1)}, f32[768]{0:T(1024)}, u32[]{:S(2)}) copy-start(f32[768]{0:T(1024)} %param.20) | copy-start | bytes 9220
  36.1 8.1 %copy-start.12 = (f32[768]{0:T(1024)S(1)}, f32[768]{0:T(1024)}, u32[]{:S(2)}) copy-start(f32[768]{0:T(1024)} %param.23) | copy-start | bytes 9220
  36.1 8.7 %copy-start.13 = (f32[768]{0:T(1024)S(1)}, f32[768]{0:T(1024)}, u32[]{:S(2)}) copy-start(f32[768]{0:T(1024)} %param.24) | copy-start | bytes 9220
  36.1 9.3 %copy-start.14 = (s32[4,8]{1,0:T(4,128)S(1)}, s32[4,8]{1,0:T(4,128)}, u32[]{:S(2)}) copy-start(s32[4,8]{1,0:T(4,128)} %param.17) | copy-start | bytes 388
  36.1 39.1 %all-to-all-start.1 = ((bf16[16,64,768]{2,1,0:T(8,128)(2,1)}), bf16[16,64,768]{2,1,0:T(8,128)(2,1)S(1)}, u32[]{:S(2)}, u32[]{:S(2)}) async-start(bf16[16,64,768]{2,1,0:T(8,128)(2,1)} %bitcast.152), calls=%async_computation.1 | async-start | bytes 3145728 | tf_op jit(solution)/shard_map/all_to_all | solution.py:387
  52.0 0.9 copy-start.17
  75.2 1.1 copy-start.5
  75.2 8.3 %copy-start.15 = (s32[4,128]{1,0:T(4,128)S(1)}, s32[4,128]{1,0:T(4,128)}, u32[]{:S(2)}) copy-start(s32[4,128]{1,0:T(4,128)} %turn.1) | copy-start | bytes 6148
  76.4 33.9 %all-to-all-start = ((bf16[16,64,768]{2,1,0:T(8,128)(2,1)}), bf16[16,64,768]{2,1,0:T(8,128)(2,1)S(1)}, u32[]{:S(2)}, u32[]{:S(2)}) async-start(bf16[16,64,768]{2,1,0:T(8,128)(2,1)} %bitcast.151), calls=%async_computation | async-start | bytes 3145728 | tf_op jit(solution)/shard_map/all_to_all | solution.py:387
  110.3 1.1 copy-start.6
  133.5 3.8 copy-start.9
  133.6 28.7 %all-to-all-start.3 = ((bf16[16,64,768]{2,1,0:T(8,128)(2,1)}), bf16[16,64,768]{2,1,0:T(8,128)(2,1)S(1)}, u32[]{:S(2)}, u32[]{:S(2)}) async-start(bf16[16,64,768]{2,1,0:T(8,128)(2,1)} %bitcast.154), calls=%async_computation.3 | async-start | bytes 3145728 | tf_op jit(solution)/shard_map/all_to_all | solution.py:387
  137.3 259.7 %reduce-scatter.5.cloned.1.call-start = ((), (), s32[]{:S(2)}) async-start(), calls=%async_computation.7 | async-start | bytes 5308416 | tf_op jit(solution)/shard_map/reduce_scatter | solution.py:505
  159.6 239.9 %reduce-scatter.3.cloned.1.call-start = ((), (), s32[]{:S(2)}) async-start(), calls=%async_computation.6 | async-start | bytes 5308416 | tf_op jit(solution)/shard_map/reduce_scatter | solution.py:504
  162.3 1.1 copy-start.7
  199.6 11.6 %copy-start.8 = (bf16[3,768,256]{2,1,0:T(8,128)(2,1)S(1)}, bf16[3,768,256]{2,1,0:T(8,128)(2,1)}, u32[]{:S(2)}) copy-start(bf16[3,768,256]{2,1,0:T(8,128)(2,1)} %get-tuple-element.64) | copy-start | bytes 3538948
  228.2 2.4 copy-start.2
  230.6 5.9 %collective-permute-start.5 = (bf16[5120,256]{1,0:T(8,128)(2,1)S(1)}, bf16[5120,256]{1,0:T(8,128)(2,1)}, u32[]{:S(2)}, u32[]{:S(2)}) collective-permute-start(bf16[5120,256]{1,0:T(8,128)(2,1)S(1)} %dynamic-slice_bitcast_fusion), channel_id=1, source_target_pairs={{0,1},{1,0},{2,3},{3,2},{4,5},{5,4},{6,7},{7,6},{8,9},{9,8},{10,11... | collective-permute-start | bytes 7864328 | tf_op jit(solution)/shard_map/ppermute | solution.py:361
  234.7 3.6 copy-start.3
  239.4 9.2 %collective-permute-start.14 = (bf16[4,160,256]{2,1,0:T(8,128)(2,1)}, bf16[4,160,256]{2,1,0:T(8,128)(2,1)}, u32[]{:S(2)}, u32[]{:S(2)}) collective-permute-start(bf16[4,160,256]{2,1,0:T(8,128)(2,1)} %get-tuple-element.126), channel_id=1, source_target_pairs={{0,96},{8,104},{16,112},{24,120},{32,0},{40,8},{48,16},{56,24},{64... | collective-permute-start | bytes 983048 | tf_op jit(solution)/shard_map/ppermute | solution.py:342
  240.9 16.9 %collective-permute-start.13 = (bf16[4,160,256]{2,1,0:T(8,128)(2,1)S(1)}, bf16[4,160,256]{2,1,0:T(8,128)(2,1)}, u32[]{:S(2)}, u32[]{:S(2)}) collective-permute-start(bf16[4,160,256]{2,1,0:T(8,128)(2,1)S(1)} %get-tuple-element.127), channel_id=1, source_target_pairs={{0,32},{8,40},{16,48},{24,56},{32,64},{40,72},{48,80},{56,88},{64,... | collective-permute-start | bytes 983048 | tf_op jit(solution)/shard_map/ppermute | solution.py:342
  240.9 16.9 %collective-permute-start.12 = (bf16[4,160,256]{2,1,0:T(8,128)(2,1)S(1)}, bf16[4,160,256]{2,1,0:T(8,128)(2,1)}, u32[]{:S(2)}, u32[]{:S(2)}) collective-permute-start(bf16[4,160,256]{2,1,0:T(8,128)(2,1)S(1)} %get-tuple-element.125), channel_id=1, source_target_pairs={{0,64},{8,72},{16,80},{24,88},{32,96},{40,104},{48,112},{56,120},{... | collective-permute-start | bytes 983048 | tf_op jit(solution)/shard_map/ppermute | solution.py:342
  243.6 17.4 %collective-permute-start.8 = (bf16[4,160,256]{2,1,0:T(8,128)(2,1)S(1)}, bf16[4,160,256]{2,1,0:T(8,128)(2,1)S(1)}, u32[]{:S(2)}, u32[]{:S(2)}) collective-permute-start(bf16[4,160,256]{2,1,0:T(8,128)(2,1)S(1)} %get-tuple-element.121), channel_id=1, source_target_pairs={{0,24},{8,0},{16,8},{24,16},{32,56},{40,32},{48,40},{56,48},{64,88... | collective-permute-start | bytes 983048 | tf_op jit(solution)/shard_map/ppermute | solution.py:342
  245.0 16.1 %collective-permute-start.7 = (bf16[4,160,256]{2,1,0:T(8,128)(2,1)S(1)}, bf16[4,160,256]{2,1,0:T(8,128)(2,1)S(1)}, u32[]{:S(2)}, u32[]{:S(2)}) collective-permute-start(bf16[4,160,256]{2,1,0:T(8,128)(2,1)S(1)} %get-tuple-element.122), channel_id=1, source_target_pairs={{0,8},{8,16},{16,24},{24,0},{32,40},{40,48},{48,56},{56,32},{64,72... | collective-permute-start | bytes 983048 | tf_op jit(solution)/shard_map/ppermute | solution.py:342
  248.6 13.0 %collective-permute-start.6 = (bf16[4,160,256]{2,1,0:T(8,128)(2,1)S(1)}, bf16[4,160,256]{2,1,0:T(8,128)(2,1)S(1)}, u32[]{:S(2)}, u32[]{:S(2)}) collective-permute-start(bf16[4,160,256]{2,1,0:T(8,128)(2,1)S(1)} %get-tuple-element.120), channel_id=1, source_target_pairs={{0,16},{8,24},{16,0},{24,8},{32,48},{40,56},{48,32},{56,40},{64,80... | collective-permute-start | bytes 983048 | tf_op jit(solution)/shard_map/ppermute | solution.py:342
  259.4 7.2 %collective-permute-start.17 = (bf16[160,256]{1,0:T(8,128)(2,1)S(1)}, bf16[160,256]{1,0:T(8,128)(2,1)S(1)}, u32[]{:S(2)}, u32[]{:S(2)}) collective-permute-start(bf16[160,256]{1,0:T(8,128)(2,1)S(1)} %get-tuple-element.156), channel_id=1, source_target_pairs={{0,24},{8,0},{16,8},{24,16},{32,56},{40,32},{48,40},{56,48},{64,88... | collective-permute-start | bytes 245768 | tf_op jit(solution)/shard_map/ppermute | solution.py:342
  259.5 8.4 %collective-permute-start.16 = (bf16[160,256]{1,0:T(8,128)(2,1)S(1)}, bf16[160,256]{1,0:T(8,128)(2,1)S(1)}, u32[]{:S(2)}, u32[]{:S(2)}) collective-permute-start(bf16[160,256]{1,0:T(8,128)(2,1)S(1)} %get-tuple-element.157), channel_id=1, source_target_pairs={{0,8},{8,16},{16,24},{24,0},{32,40},{40,48},{48,56},{56,32},{64,72... | collective-permute-start | bytes 245768 | tf_op jit(solution)/shard_map/ppermute | solution.py:342
  261.0 7.0 %collective-permute-start.15 = (bf16[160,256]{1,0:T(8,128)(2,1)S(1)}, bf16[160,256]{1,0:T(8,128)(2,1)S(1)}, u32[]{:S(2)}, u32[]{:S(2)}) collective-permute-start(bf16[160,256]{1,0:T(8,128)(2,1)S(1)} %get-tuple-element.155), channel_id=1, source_target_pairs={{0,16},{8,24},{16,0},{24,8},{32,48},{40,56},{48,32},{56,40},{64,80... | collective-permute-start | bytes 245768 | tf_op jit(solution)/shard_map/ppermute | solution.py:342
  262.8 5.3 %collective-permute-start.11 = (bf16[160,256]{1,0:T(8,128)(2,1)S(1)}, bf16[160,256]{1,0:T(8,128)(2,1)S(1)}, u32[]{:S(2)}, u32[]{:S(2)}) collective-permute-start(bf16[160,256]{1,0:T(8,128)(2,1)S(1)} %get-tuple-element.153), channel_id=1, source_target_pairs={{0,96},{8,104},{16,112},{24,120},{32,0},{40,8},{48,16},{56,24},{64... | collective-permute-start | bytes 245768 | tf_op jit(solution)/shard_map/ppermute | solution.py:342
  266.7 5.8 %collective-permute-start.10 = (bf16[160,256]{1,0:T(8,128)(2,1)S(1)}, bf16[160,256]{1,0:T(8,128)(2,1)S(1)}, u32[]{:S(2)}, u32[]{:S(2)}) collective-permute-start(bf16[160,256]{1,0:T(8,128)(2,1)S(1)} %get-tuple-element.154), channel_id=1, source_target_pairs={{0,32},{8,40},{16,48},{24,56},{32,64},{40,72},{48,80},{56,88},{64,... | collective-permute-start | bytes 245768 | tf_op jit(solution)/shard_map/ppermute | solution.py:342
  266.7 5.8 %collective-permute-start.9 = (bf16[160,256]{1,0:T(8,128)(2,1)S(1)}, bf16[160,256]{1,0:T(8,128)(2,1)S(1)}, u32[]{:S(2)}, u32[]{:S(2)}) collective-permute-start(bf16[160,256]{1,0:T(8,128)(2,1)S(1)} %get-tuple-element.152), channel_id=1, source_target_pairs={{0,64},{8,72},{16,80},{24,88},{32,96},{40,104},{48,112},{56,120},{... | collective-permute-start | bytes 245768 | tf_op jit(solution)/shard_map/ppermute | solution.py:342
  272.5 9.1 %collective-permute-start.20 = (bf16[2,160,256]{2,1,0:T(8,128)(2,1)S(1)}, bf16[2,160,256]{2,1,0:T(8,128)(2,1)S(1)}, u32[]{:S(2)}, u32[]{:S(2)}) collective-permute-start(bf16[2,160,256]{2,1,0:T(8,128)(2,1)S(1)} %pad_maximum_fusion.8), channel_id=1, source_target_pairs={{0,6},{1,7},{2,0},{3,1},{4,2},{5,3},{6,4},{7,5},{8,14},{9,15},{10,... | collective-permute-start | bytes 491528 | tf_op jit(solution)/shard_map/ppermute | solution.py:342
  276.6 8.4 %collective-permute-start.19 = (bf16[2,160,256]{2,1,0:T(8,128)(2,1)S(1)}, bf16[2,160,256]{2,1,0:T(8,128)(2,1)S(1)}, u32[]{:S(2)}, u32[]{:S(2)}) collective-permute-start(bf16[2,160,256]{2,1,0:T(8,128)(2,1)S(1)} %pad_maximum_fusion.8), channel_id=1, source_target_pairs={{0,2},{1,3},{2,4},{3,5},{4,6},{5,7},{6,0},{7,1},{8,10},{9,11},{10,... | collective-permute-start | bytes 491528 | tf_op jit(solution)/shard_map/ppermute | solution.py:342
  276.6 8.4 %collective-permute-start.18 = (bf16[2,160,256]{2,1,0:T(8,128)(2,1)S(1)}, bf16[2,160,256]{2,1,0:T(8,128)(2,1)S(1)}, u32[]{:S(2)}, u32[]{:S(2)}) collective-permute-start(bf16[2,160,256]{2,1,0:T(8,128)(2,1)S(1)} %pad_maximum_fusion.8), channel_id=1, source_target_pairs={{0,4},{1,5},{2,6},{3,7},{4,0},{5,1},{6,2},{7,3},{8,12},{9,13},{10,... | collective-permute-start | bytes 491528 | tf_op jit(solution)/shard_map/ppermute | solution.py:342
  285.1 6.6 %collective-permute-start.23 = (bf16[160,256]{1,0:T(8,128)(2,1)S(1)}, bf16[160,256]{1,0:T(8,128)(2,1)S(1)}, u32[]{:S(2)}, u32[]{:S(2)}) collective-permute-start(bf16[160,256]{1,0:T(8,128)(2,1)S(1)} %get-tuple-element.159), channel_id=1, source_target_pairs={{0,96},{8,104},{16,112},{24,120},{32,0},{40,8},{48,16},{56,24},{64... | collective-permute-start | bytes 245768 | tf_op jit(solution)/shard_map/ppermute | solution.py:350
  287.5 4.9 %collective-permute-start.22 = (bf16[160,256]{1,0:T(8,128)(2,1)S(1)}, bf16[160,256]{1,0:T(8,128)(2,1)S(1)}, u32[]{:S(2)}, u32[]{:S(2)}) collective-permute-start(bf16[160,256]{1,0:T(8,128)(2,1)S(1)} %get-tuple-element.159), channel_id=1, source_target_pairs={{0,64},{8,72},{16,80},{24,88},{32,96},{40,104},{48,112},{56,120},{... | collective-permute-start | bytes 245768 | tf_op jit(solution)/shard_map/ppermute | solution.py:350
  287.7 5.4 %collective-permute-start.21 = (bf16[160,256]{1,0:T(8,128)(2,1)S(1)}, bf16[160,256]{1,0:T(8,128)(2,1)S(1)}, u32[]{:S(2)}, u32[]{:S(2)}) collective-permute-start(bf16[160,256]{1,0:T(8,128)(2,1)S(1)} %get-tuple-element.159), channel_id=1, source_target_pairs={{0,32},{8,40},{16,48},{24,56},{32,64},{40,72},{48,80},{56,88},{64,... | collective-permute-start | bytes 245768 | tf_op jit(solution)/shard_map/ppermute | solution.py:350
  288.1 8.2 %collective-permute-start.29 = (bf16[160,256]{1,0:T(8,128)(2,1)S(1)}, bf16[160,256]{1,0:T(8,128)(2,1)S(1)}, u32[]{:S(2)}, u32[]{:S(2)}) collective-permute-start(bf16[160,256]{1,0:T(8,128)(2,1)S(1)} %get-tuple-element.160), channel_id=1, source_target_pairs={{0,24},{8,0},{16,8},{24,16},{32,56},{40,32},{48,40},{56,48},{64,88... | collective-permute-start | bytes 245768 | tf_op jit(solution)/shard_map/ppermute | solution.py:350
  291.0 5.9 %collective-permute-start.28 = (bf16[160,256]{1,0:T(8,128)(2,1)S(1)}, bf16[160,256]{1,0:T(8,128)(2,1)S(1)}, u32[]{:S(2)}, u32[]{:S(2)}) collective-permute-start(bf16[160,256]{1,0:T(8,128)(2,1)S(1)} %get-tuple-element.160), channel_id=1, source_target_pairs={{0,16},{8,24},{16,0},{24,8},{32,48},{40,56},{48,32},{56,40},{64,80... | collective-permute-start | bytes 245768 | tf_op jit(solution)/shard_map/ppermute | solution.py:350
  291.6 5.3 %collective-permute-start.27 = (bf16[160,256]{1,0:T(8,128)(2,1)S(1)}, bf16[160,256]{1,0:T(8,128)(2,1)S(1)}, u32[]{:S(2)}, u32[]{:S(2)}) collective-permute-start(bf16[160,256]{1,0:T(8,128)(2,1)S(1)} %get-tuple-element.160), channel_id=1, source_target_pairs={{0,8},{8,16},{16,24},{24,0},{32,40},{40,48},{48,56},{56,32},{64,72... | collective-permute-start | bytes 245768 | tf_op jit(solution)/shard_map/ppermute | solution.py:350
  293.2 12.0 %collective-permute-start.26 = (bf16[4,160,256]{2,1,0:T(8,128)(2,1)S(1)}, bf16[4,160,256]{2,1,0:T(8,128)(2,1)S(1)}, u32[]{:S(2)}, u32[]{:S(2)}) collective-permute-start(bf16[4,160,256]{2,1,0:T(8,128)(2,1)S(1)} %get-tuple-element.141), channel_id=1, source_target_pairs={{0,24},{8,0},{16,8},{24,16},{32,56},{40,32},{48,40},{56,48},{64,88... | collective-permute-start | bytes 983048 | tf_op jit(solution)/shard_map/ppermute | solution.py:350
  295.8 9.4 %collective-permute-start.25 = (bf16[4,160,256]{2,1,0:T(8,128)(2,1)S(1)}, bf16[4,160,256]{2,1,0:T(8,128)(2,1)S(1)}, u32[]{:S(2)}, u32[]{:S(2)}) collective-permute-start(bf16[4,160,256]{2,1,0:T(8,128)(2,1)S(1)} %get-tuple-element.141), channel_id=1, source_target_pairs={{0,16},{8,24},{16,0},{24,8},{32,48},{40,56},{48,32},{56,40},{64,80... | collective-permute-start | bytes 983048 | tf_op jit(solution)/shard_map/ppermute | solution.py:350
  296.3 12.9 %collective-permute-start.24 = (bf16[4,160,256]{2,1,0:T(8,128)(2,1)S(1)}, bf16[4,160,256]{2,1,0:T(8,128)(2,1)S(1)}, u32[]{:S(2)}, u32[]{:S(2)}) collective-permute-start(bf16[4,160,256]{2,1,0:T(8,128)(2,1)S(1)} %get-tuple-element.141), channel_id=1, source_target_pairs={{0,8},{8,16},{16,24},{24,0},{32,40},{40,48},{48,56},{56,32},{64,72... | collective-permute-start | bytes 983048 | tf_op jit(solution)/shard_map/ppermute | solution.py:350
  297.1 12.4 %collective-permute-start.32 = (bf16[4,160,256]{2,1,0:T(8,128)(2,1)S(1)}, bf16[4,160,256]{2,1,0:T(8,128)(2,1)S(1)}, u32[]{:S(2)}, u32[]{:S(2)}) collective-permute-start(bf16[4,160,256]{2,1,0:T(8,128)(2,1)S(1)} %get-tuple-element.147), channel_id=1, source_target_pairs={{0,96},{8,104},{16,112},{24,120},{32,0},{40,8},{48,16},{56,24},{64... | collective-permute-start | bytes 983048 | tf_op jit(solution)/shard_map/ppermute | solution.py:350
  299.4 10.1 %collective-permute-start.31 = (bf16[4,160,256]{2,1,0:T(8,128)(2,1)S(1)}, bf16[4,160,256]{2,1,0:T(8,128)(2,1)S(1)}, u32[]{:S(2)}, u32[]{:S(2)}) collective-permute-start(bf16[4,160,256]{2,1,0:T(8,128)(2,1)S(1)} %get-tuple-element.147), channel_id=1, source_target_pairs={{0,64},{8,72},{16,80},{24,88},{32,96},{40,104},{48,112},{56,120},{... | collective-permute-start | bytes 983048 | tf_op jit(solution)/shard_map/ppermute | solution.py:350
  305.2 7.4 %collective-permute-start.30 = (bf16[4,160,256]{2,1,0:T(8,128)(2,1)S(1)}, bf16[4,160,256]{2,1,0:T(8,128)(2,1)S(1)}, u32[]{:S(2)}, u32[]{:S(2)}) collective-permute-start(bf16[4,160,256]{2,1,0:T(8,128)(2,1)S(1)} %get-tuple-element.147), channel_id=1, source_target_pairs={{0,32},{8,40},{16,48},{24,56},{32,64},{40,72},{48,80},{56,88},{64,... | collective-permute-start | bytes 983048 | tf_op jit(solution)/shard_map/ppermute | solution.py:350
  313.5 46.4 %collective-permute-start.33 = (bf16[5120,256]{1,0:T(8,128)(2,1)S(1)}, bf16[5120,256]{1,0:T(8,128)(2,1)}, u32[]{:S(2)}, u32[]{:S(2)}) collective-permute-start(bf16[5120,256]{1,0:T(8,128)(2,1)S(1)} %bitcast.133), channel_id=1, source_target_pairs={{0,1},{1,0},{2,3},{3,2},{4,5},{5,4},{6,7},{7,6},{8,9},{9,8},{10,11... | collective-permute-start | bytes 7864328 | tf_op jit(solution)/shard_map/ppermute | solution.py:381
  321.8 5.7 %collective-permute-start.3 = (bf16[4,128,768]{2,1,0:T(8,128)(2,1)}, bf16[4,128,768]{2,1,0:T(8,128)(2,1)S(1)}, u32[]{:S(2)}, u32[]{:S(2)}) collective-permute-start(bf16[4,128,768]{2,1,0:T(8,128)(2,1)} %get-tuple-element.59), channel_id=1, source_target_pairs={{0,1},{1,0},{2,3},{3,2},{4,5},{5,4},{6,7},{7,6},{8,9},{9,8},{10,11... | collective-permute-start | bytes 2359304 | tf_op jit(solution)/shard_map/ppermute | solution.py:546
  321.9 29.1 %all-to-all-start.2 = ((bf16[16,64,768]{2,1,0:T(8,128)(2,1)}), bf16[16,64,768]{2,1,0:T(8,128)(2,1)}, u32[]{:S(2)}, u32[]{:S(2)}) async-start(bf16[16,64,768]{2,1,0:T(8,128)(2,1)} %bitcast.146), calls=%async_computation.2 | async-start | bytes 3145728 | tf_op jit(solution)/shard_map/all_to_all | solution.py:387
  327.5 27.4 %copy-start.4 = (bf16[4,128,768]{2,1,0:T(8,128)(2,1)}, bf16[4,128,768]{2,1,0:T(8,128)(2,1)S(1)}, u32[]{:S(2)}) copy-start(bf16[4,128,768]{2,1,0:T(8,128)(2,1)S(1)} %collective-permute-done.3) | copy-start | bytes 2359300
  329.9 25.0 %collective-permute-start.4 = (bf16[4,128,768]{2,1,0:T(8,128)(2,1)}, bf16[4,128,768]{2,1,0:T(8,128)(2,1)}, u32[]{:S(2)}, u32[]{:S(2)}) collective-permute-start(bf16[4,128,768]{2,1,0:T(8,128)(2,1)} %add_select_fusion), channel_id=1, source_target_pairs={{2,0},{3,1},{4,2},{5,3},{6,4},{7,5},{10,8},{11,9},{12,10},{13,11},... | collective-permute-start | bytes 2359304 | tf_op jit(solution)/shard_map/ppermute | solution.py:548
  363.8 7.3 %copy-start.1 = (bf16[2,5120,256]{2,1,0:T(8,128)(2,1)}, bf16[2,5120,256]{2,1,0:T(8,128)(2,1)S(1)}, u32[]{:S(2)}) copy-start(bf16[2,5120,256]{2,1,0:T(8,128)(2,1)S(1)} %maximum_select_fusion) | copy-start | bytes 15728644
  364.6 6.1 %copy-start = (f32[9216,256]{1,0:T(8,128)}, f32[9216,256]{1,0:T(8,128)S(1)}, u32[]{:S(2)}) copy-start(f32[9216,256]{1,0:T(8,128)S(1)} %slice_convert_fusion) | copy-start | bytes 28311556
  380.4 8.1 %slice-start = ((f32[9216,256]{1,0:T(8,128)}), f32[2304,256]{1,0:T(8,128)S(1)}, s32[]{:S(2)}) async-start(f32[9216,256]{1,0:T(8,128)} %copy-done), calls=%async_computation.8 | async-start | bytes 4718592 | tf_op jit(solution)/shard_map/slice | solution.py:569
Sparse Core Ops, SparseCore 0:
  159.8 38.9 reduce-scatter.4
  242.3 37.9 reduce-scatter.2
